TPU v7x, 32 devices: a whole 2x2x4 slice. The times are simulated.
32 devices in a mesh: ctx: 4 (over x, core), fsdp: 8 (over z, y).
Axes of the slice: x: 2, y: 2, z: 4, core: 2. Of those that a mesh axis runs over, the one named last changes fastest.
Arguments:
- hidden_in: bfloat16 [8, 2048, 576], P('fsdp', 'ctx'), may hold values from -41 to 41
- positions: int32 [8, 2048], P('fsdp', 'ctx'), may hold values from 0 to 2047, as said below
- out_grad: bfloat16 [8, 2048, 576], P('fsdp', 'ctx'), may hold values from -6 to 6
- attn_gain: bfloat16 [576], P('fsdp'), may hold values from 0.099609375 to 1.8984375
- query_weight: bfloat16 [576, 576], P('fsdp'), may hold values from -0.25 to 0.25
- key_matrix: bfloat16 [576, 192], P('fsdp'), may hold values from -0.25 to 0.25
- value_matrix: bfloat16 [576, 192], P('fsdp'), may hold values from -0.25 to 0.25
- out_weight: bfloat16 [576, 576], P(None, 'fsdp'), may hold values from -3 to 3
- mlp_gain: bfloat16 [576], P('fsdp'), may hold values from 0.099609375 to 1.8984375
- gate_weight: bfloat16 [576, 1536], P(None, 'fsdp'), may hold values from -0.25 to 0.25
- up_weight: bfloat16 [576, 1536], P(None, 'fsdp'), may hold values from -0.25 to 0.25
- down_weight: bfloat16 [1536, 576], P('fsdp'), may hold values from -0.15625 to 0.15625
Outputs:
- hidden_out: bfloat16 [8, 2048, 576], P('fsdp', 'ctx')
- input_grad: float32 [8, 2048, 576], P('fsdp', 'ctx')
- attn_gain_grad: float32 [576], P('fsdp')
- query_weight_grad: float32 [576, 576], P('fsdp')
- key_weight_grad: float32 [576, 192], P('fsdp')
- value_weight_grad: float32 [576, 192], P('fsdp')
- out_weight_grad: float32 [576, 576], P(None, 'fsdp')
- mlp_gain_grad: float32 [576], P('fsdp')
- gate_weight_grad: float32 [576, 1536], P(None, 'fsdp')
- up_weight_grad: float32 [576, 1536], P(None, 'fsdp')
- down_weight_grad: float32 [1536, 576], P('fsdp')
Inputs may be any that keep to these rules, and one draw needn't show every extreme that they name: Each row is a permutation of the positions of its sequence, made of runs of 256 consecutive rising positions that start at multiples of 256, the runs in an order drawn from the seed.
All inputs are finite; a program needn't handle non-finite values.
Results may differ from a plain program's by a relative error of at most 0.028.
Values may be sent and summed in bfloat16 or wider, within the bound.
No kernel may reach another device: no remote copies, remote signals or barrier semaphores. Data moves between devices by JAX's collectives and lax.ppermute only.
A program may use at most 128 MiB of HBM per device.

v0:
```python
import math

import jax
import jax.numpy as jnp
from jax import lax
from jax.sharding import PartitionSpec as P

QUERY_HEADS = 9
KEY_VALUE_HEADS = 3
HEAD_FEATURES = 64


rms_epsilon = 1e-05
rope_base = 100000.0
score_after_mask = -1e30


def from_behind(value, axis, steps):
    count = lax.axis_size(axis)
    pairs = [(source, (source + steps) % count) for source in range(count)]
    return lax.ppermute(value, axis, pairs)


def rope_tables(places):
    half_dim = HEAD_FEATURES // 2
    frequencies = rope_base ** (-jnp.arange(half_dim, dtype=jnp.float32) / half_dim)
    angles = places.astype(jnp.float32)[:, None] * frequencies[None, :]
    return (jnp.cos(angles)[:, None, :], jnp.sin(angles)[:, None, :])


def apply_rotation(vectors, cosine_table, sine_values):
    half_dim = HEAD_FEATURES // 2
    first_half = vectors[..., :half_dim]
    second_half = vectors[..., half_dim:]
    return jnp.concatenate(
        [
            first_half * cosine_table - second_half * sine_values,
            second_half * cosine_table + first_half * sine_values,
        ],
        axis=-1,
    )


def reverse_rotation(grads_rot, cosine_table, sine_values):
    half_dim = HEAD_FEATURES // 2
    first_half = grads_rot[..., :half_dim]
    second_half = grads_rot[..., half_dim:]
    return jnp.concatenate(
        [
            first_half * cosine_table + second_half * sine_values,
            second_half * cosine_table - first_half * sine_values,
        ],
        axis=-1,
    )


def norm_forward(value_rows, gain_row):
    scale_row = lax.rsqrt(jnp.mean(value_rows * value_rows, axis=-1, keepdims=True) + rms_epsilon)
    return (value_rows * scale_row * gain_row, scale_row)


def norm_backward(value_rows, scale_row, gain_row, grad_normed):
    unit_rows = value_rows * scale_row
    grad_unit = grad_normed * gain_row
    values_gradient = scale_row * (
        grad_unit - unit_rows * jnp.mean(grad_unit * unit_rows, axis=-1, keepdims=True)
    )
    return (values_gradient, jnp.sum(grad_normed * unit_rows, axis=0))


def attention_weights(attn_gain, query_weight, key_matrix, value_matrix, out_weight):
    return (
        lax.all_gather(attn_gain, "fsdp", axis=0, tiled=True),
        lax.all_gather(query_weight, "fsdp", axis=0, tiled=True),
        lax.all_gather(key_matrix, "fsdp", axis=0, tiled=True),
        lax.all_gather(value_matrix, "fsdp", axis=0, tiled=True),
        lax.all_gather(out_weight, "fsdp", axis=1, tiled=True),
    )


def feed_weights(mlp_gain, gate_weight, up_weight, down_weight):
    return (
        lax.all_gather(mlp_gain, "fsdp", axis=0, tiled=True),
        lax.all_gather(gate_weight, "fsdp", axis=1, tiled=True),
        lax.all_gather(up_weight, "fsdp", axis=1, tiled=True),
        lax.all_gather(down_weight, "fsdp", axis=0, tiled=True),
    )


def head_scores(query_head, key_head, query_places, key_places):
    raw_scores = jnp.einsum(
        "tgd,sd->gts", query_head, key_head, preferred_element_type=jnp.float32
    ) * (1.0 / math.sqrt(HEAD_FEATURES))
    visible = key_places[None, None, :] <= query_places[None, :, None]
    return jnp.where(visible, raw_scores, score_after_mask)


def split_block(key_value_block):
    rows_per_block = key_value_block.shape[0]
    key_head_rows = (
        key_value_block[:, : KEY_VALUE_HEADS * HEAD_FEATURES]
        .reshape(rows_per_block, KEY_VALUE_HEADS, HEAD_FEATURES)
        .transpose(1, 0, 2)
    )
    value_head_rows = (
        key_value_block[:, KEY_VALUE_HEADS * HEAD_FEATURES :]
        .reshape(rows_per_block, KEY_VALUE_HEADS, HEAD_FEATURES)
        .transpose(1, 0, 2)
    )
    return (key_head_rows, value_head_rows)


def online_step(query_head_rows, query_places):

    def update(carried, key_value_block, key_places):
        key_head_rows, value_head_rows = split_block(key_value_block)

        def per_head(pieces):
            query_head, key_head, value_head, maxima, totals, partial_value = pieces
            scores = head_scores(query_head, key_head, query_places, key_places)
            new_maxima = jnp.maximum(maxima, jnp.max(scores, axis=-1))
            factor = jnp.exp(maxima - new_maxima)
            weights_now = jnp.exp(scores - new_maxima[..., None])
            totals = totals * factor + jnp.sum(weights_now, axis=-1)
            partial_value = partial_value * factor[..., None] + jnp.einsum(
                "gts,sd->gtd",
                weights_now.astype(jnp.bfloat16),
                value_head,
                preferred_element_type=jnp.float32,
            )
            return (new_maxima, totals, partial_value)

        return lax.map(
            per_head,
            (query_head_rows, key_head_rows, value_head_rows, carried[0], carried[1], carried[2]),
        )

    return update


def grad_step(query_head_rows, query_places, log_totals, heads_gradient, deltas):

    def update(carried, key_value_block, key_places):
        rows_per_block = key_value_block.shape[0]
        key_head_rows, value_head_rows = split_block(key_value_block)

        def per_head(pieces):
            query_head, key_head, value_head, head_log_total, grad_head, head_delta, grad_query = (
                pieces
            )
            scores = head_scores(query_head, key_head, query_places, key_places)
            probabilities = jnp.exp(scores - head_log_total[..., None])
            value_gradient = jnp.einsum(
                "gts,tgd->sd",
                probabilities.astype(jnp.bfloat16),
                grad_head,
                preferred_element_type=jnp.float32,
            )
            grad_probs = jnp.einsum(
                "tgd,sd->gts", grad_head, value_head, preferred_element_type=jnp.float32
            )
            grad_scores = (
                probabilities
                * (grad_probs - head_delta[..., None])
                * (1.0 / math.sqrt(HEAD_FEATURES))
            ).astype(jnp.bfloat16)
            grad_query = grad_query + jnp.einsum(
                "gts,sd->tgd", grad_scores, key_head, preferred_element_type=jnp.float32
            )
            key_gradient = jnp.einsum(
                "gts,tgd->sd", grad_scores, query_head, preferred_element_type=jnp.float32
            )
            return (grad_query, key_gradient, value_gradient)

        grad_query, key_gradient, value_gradient = lax.map(
            per_head,
            (
                query_head_rows,
                key_head_rows,
                value_head_rows,
                log_totals,
                heads_gradient,
                deltas,
                carried,
            ),
        )
        block_grads = jnp.concatenate(
            [
                key_gradient.transpose(1, 0, 2).reshape(
                    rows_per_block, KEY_VALUE_HEADS * HEAD_FEATURES
                ),
                value_gradient.transpose(1, 0, 2).reshape(
                    rows_per_block, KEY_VALUE_HEADS * HEAD_FEATURES
                ),
            ],
            axis=-1,
        )
        return (grad_query, block_grads)

    return update


def maybe_skip(update):

    def guarded(carried, key_value_block, key_places):
        return update(carried, key_value_block, key_places)

    return guarded


def visit_blocks(update, carried, local_block, key_places, my_index, axis_count):
    rows_per_block = local_block.shape[0]
    carried = update(
        carried,
        local_block,
        lax.dynamic_slice_in_dim(key_places, my_index * rows_per_block, rows_per_block),
    )

    def advance(step_index, loop_state):
        key_value_block, running = loop_state
        key_value_block = from_behind(key_value_block, "ctx", 1)
        source = (my_index - step_index) % axis_count
        running = update(
            running,
            key_value_block,
            lax.dynamic_slice_in_dim(key_places, source * rows_per_block, rows_per_block),
        )
        return (key_value_block, running)

    return lax.fori_loop(1, axis_count, advance, (local_block, carried))[1]


def pass_grads(moving_grads):
    return from_behind(moving_grads.astype(jnp.bfloat16), "ctx", 1).astype(moving_grads.dtype)


def visit_back(update, carried, local_block, key_places, my_index, axis_count):
    rows_per_block = local_block.shape[0]
    carried, moving_grads = update(
        carried,
        local_block,
        lax.dynamic_slice_in_dim(key_places, my_index * rows_per_block, rows_per_block),
    )

    def advance(step_index, loop_state):
        key_value_block, moving, running = loop_state
        key_value_block = from_behind(key_value_block, "ctx", 1)
        moving = pass_grads(moving)
        source = (my_index - step_index) % axis_count
        running, added_grads = update(
            running,
            key_value_block,
            lax.dynamic_slice_in_dim(key_places, source * rows_per_block, rows_per_block),
        )
        return (key_value_block, moving + added_grads, running)

    loop_state = lax.fori_loop(1, axis_count, advance, (local_block, moving_grads, carried))
    return (loop_state[2], pass_grads(loop_state[1]))


def on_device(
    hidden_in,
    positions,
    out_grad,
    attn_gain,
    query_weight,
    key_matrix,
    value_matrix,
    out_weight,
    mlp_gain,
    gate_weight,
    up_weight,
    down_weight,
):
    count_of_tokens = hidden_in.shape[1]
    heads_per_group = QUERY_HEADS // KEY_VALUE_HEADS
    my_index = lax.axis_index("ctx")
    axis_count = lax.axis_size("ctx")
    hidden = hidden_in[0].astype(jnp.float32)
    query_places = positions[0]
    key_places = lax.all_gather(query_places, "ctx", axis=0, tiled=True)
    cosine_table, sine_values = rope_tables(query_places)
    full_attn_gain, full_query, full_key, full_value, full_out = attention_weights(
        attn_gain, query_weight, key_matrix, value_matrix, out_weight
    )
    attn_scale = full_attn_gain.astype(jnp.float32)
    normed_value, attn_rms = norm_forward(hidden, attn_scale)
    attention_normed = normed_value.astype(jnp.bfloat16)
    query_pre = jnp.dot(attention_normed, full_query, preferred_element_type=jnp.float32).reshape(
        count_of_tokens, QUERY_HEADS, HEAD_FEATURES
    )
    query_rows = apply_rotation(query_pre, cosine_table, sine_values).astype(jnp.bfloat16)
    query_head_rows = query_rows.reshape(
        count_of_tokens, KEY_VALUE_HEADS, heads_per_group, HEAD_FEATURES
    ).transpose(1, 0, 2, 3)
    key_before_rotation = jnp.dot(
        attention_normed, full_key, preferred_element_type=jnp.float32
    ).reshape(count_of_tokens, KEY_VALUE_HEADS, HEAD_FEATURES)
    rotated_keys = apply_rotation(key_before_rotation, cosine_table, sine_values).astype(
        jnp.bfloat16
    )
    local_value_rows = jnp.dot(
        attention_normed, full_value, preferred_element_type=jnp.float32
    ).astype(jnp.bfloat16)
    local_block = jnp.concatenate(
        [rotated_keys.reshape(count_of_tokens, KEY_VALUE_HEADS * HEAD_FEATURES), local_value_rows],
        axis=-1,
    )
    initial_maximum = jnp.full(
        (KEY_VALUE_HEADS, heads_per_group, count_of_tokens), score_after_mask, jnp.float32
    )
    initial_total = jnp.zeros((KEY_VALUE_HEADS, heads_per_group, count_of_tokens), jnp.float32)
    initial_sum = jnp.zeros(
        (KEY_VALUE_HEADS, heads_per_group, count_of_tokens, HEAD_FEATURES), jnp.float32
    )
    maxima, totals, partial_value = visit_blocks(
        maybe_skip(online_step(query_head_rows, query_places)),
        (initial_maximum, initial_total, initial_sum),
        local_block,
        key_places,
        my_index,
        axis_count,
    )
    log_totals = maxima + jnp.log(totals)
    partial_value = partial_value / totals[..., None]
    attended = partial_value.transpose(2, 0, 1, 3).reshape(
        count_of_tokens, QUERY_HEADS * HEAD_FEATURES
    )
    attended_low = attended.astype(jnp.bfloat16)
    middle = hidden + jnp.dot(attended_low, full_out, preferred_element_type=jnp.float32)
    full_mlp_gain, full_gate, full_up, full_down = feed_weights(
        mlp_gain, gate_weight, up_weight, down_weight
    )
    mlp_scale = full_mlp_gain.astype(jnp.float32)
    normed_second, mlp_rms = norm_forward(middle, mlp_scale)
    normed_mlp = normed_second.astype(jnp.bfloat16)
    gate_value = jnp.dot(normed_mlp, full_gate, preferred_element_type=jnp.float32)
    up_value = jnp.dot(normed_mlp, full_up, preferred_element_type=jnp.float32)
    sigmoid_gate = jax.nn.sigmoid(gate_value)
    silu_gate = gate_value * sigmoid_gate
    activated = (silu_gate * up_value).astype(jnp.bfloat16)
    result = middle + jnp.dot(activated, full_down, preferred_element_type=jnp.float32)
    hidden_out = result.astype(jnp.bfloat16)
    grad_out_low = out_grad[0]
    grad_out = grad_out_low.astype(jnp.float32)
    full_mlp_gain, full_gate, full_up, full_down = feed_weights(
        mlp_gain, gate_weight, up_weight, down_weight
    )
    grad_down_w = jnp.einsum(
        "tf,td->fd", activated, grad_out_low, preferred_element_type=jnp.float32
    )
    grad_act = jnp.einsum("td,fd->tf", grad_out_low, full_down, preferred_element_type=jnp.float32)
    grad_gate = (
        grad_act * up_value * sigmoid_gate * (1.0 + gate_value * (1.0 - sigmoid_gate))
    ).astype(jnp.bfloat16)
    grad_up = (grad_act * silu_gate).astype(jnp.bfloat16)
    grad_gate_w = jnp.einsum("td,tf->df", normed_mlp, grad_gate, preferred_element_type=jnp.float32)
    grad_up_w = jnp.einsum("td,tf->df", normed_mlp, grad_up, preferred_element_type=jnp.float32)
    grad_normed_mlp = jnp.einsum(
        "tf,df->td", grad_gate, full_gate, preferred_element_type=jnp.float32
    ) + jnp.einsum("tf,df->td", grad_up, full_up, preferred_element_type=jnp.float32)
    grad_middle_norm, grad_mlp_gain = norm_backward(
        middle, mlp_rms, full_mlp_gain.astype(jnp.float32), grad_normed_mlp
    )
    grad_middle = grad_out + grad_middle_norm
    feed_grads = (
        lax.psum_scatter(
            grad_mlp_gain.astype(jnp.bfloat16), "fsdp", scatter_dimension=0, tiled=True
        ).astype(jnp.float32),
        lax.psum_scatter(
            grad_gate_w.astype(jnp.bfloat16), "fsdp", scatter_dimension=1, tiled=True
        ).astype(jnp.float32),
        lax.psum_scatter(
            grad_up_w.astype(jnp.bfloat16), "fsdp", scatter_dimension=1, tiled=True
        ).astype(jnp.float32),
        lax.psum_scatter(
            grad_down_w.astype(jnp.bfloat16), "fsdp", scatter_dimension=0, tiled=True
        ).astype(jnp.float32),
    )
    feed_grads = (
        lax.psum(feed_grads[0].astype(jnp.bfloat16), "ctx").astype(jnp.float32),
        lax.psum(feed_grads[1].astype(jnp.bfloat16), "ctx").astype(jnp.float32),
        lax.psum(feed_grads[2].astype(jnp.bfloat16), "ctx").astype(jnp.float32),
        lax.psum(feed_grads[3].astype(jnp.bfloat16), "ctx").astype(jnp.float32),
    )
    full_attn_gain, full_query, full_key, full_value, full_out = attention_weights(
        attn_gain, query_weight, key_matrix, value_matrix, out_weight
    )
    grad_middle_low = grad_middle.astype(jnp.bfloat16)
    grad_out_w = jnp.einsum(
        "tc,td->cd", attended_low, grad_middle_low, preferred_element_type=jnp.float32
    )
    attended_gradient = jnp.einsum(
        "td,cd->tc", grad_middle_low, full_out, preferred_element_type=jnp.float32
    ).astype(jnp.bfloat16)
    deltas = (
        (attended_gradient.astype(jnp.float32) * attended)
        .reshape(count_of_tokens, KEY_VALUE_HEADS, heads_per_group, HEAD_FEATURES)
        .sum(axis=-1)
        .transpose(1, 2, 0)
    )
    heads_gradient = attended_gradient.reshape(
        count_of_tokens, KEY_VALUE_HEADS, heads_per_group, HEAD_FEATURES
    ).transpose(1, 0, 2, 3)
    initial_gradient = jnp.zeros(
        (KEY_VALUE_HEADS, count_of_tokens, heads_per_group, HEAD_FEATURES), jnp.float32
    )
    grad_query_heads, block_gradient = visit_back(
        maybe_skip(grad_step(query_head_rows, query_places, log_totals, heads_gradient, deltas)),
        initial_gradient,
        local_block,
        key_places,
        my_index,
        axis_count,
    )
    grad_queries = (
        reverse_rotation(
            grad_query_heads.transpose(1, 0, 2, 3).reshape(
                count_of_tokens, QUERY_HEADS, HEAD_FEATURES
            ),
            cosine_table,
            sine_values,
        )
        .astype(jnp.bfloat16)
        .reshape(count_of_tokens, QUERY_HEADS * HEAD_FEATURES)
    )
    grad_keys = (
        reverse_rotation(
            block_gradient[:, : KEY_VALUE_HEADS * HEAD_FEATURES].reshape(
                count_of_tokens, KEY_VALUE_HEADS, HEAD_FEATURES
            ),
            cosine_table,
            sine_values,
        )
        .astype(jnp.bfloat16)
        .reshape(count_of_tokens, KEY_VALUE_HEADS * HEAD_FEATURES)
    )
    values_gradient = block_gradient[:, KEY_VALUE_HEADS * HEAD_FEATURES :].astype(jnp.bfloat16)
    grad_query_w = jnp.einsum(
        "td,tc->dc", attention_normed, grad_queries, preferred_element_type=jnp.float32
    )
    grad_key_w = jnp.einsum(
        "td,tc->dc", attention_normed, grad_keys, preferred_element_type=jnp.float32
    )
    grad_value_w = jnp.einsum(
        "td,tc->dc", attention_normed, values_gradient, preferred_element_type=jnp.float32
    )
    grad_normed_attn = jnp.einsum(
        "tc,dc->td", grad_queries, full_query, preferred_element_type=jnp.float32
    )
    grad_normed_attn = grad_normed_attn + jnp.einsum(
        "tc,dc->td", grad_keys, full_key, preferred_element_type=jnp.float32
    )
    grad_normed_attn = grad_normed_attn + jnp.einsum(
        "tc,dc->td", values_gradient, full_value, preferred_element_type=jnp.float32
    )
    grad_hidden_norm, grad_attn_gain = norm_backward(
        hidden, attn_rms, full_attn_gain.astype(jnp.float32), grad_normed_attn
    )
    input_grad = grad_middle + grad_hidden_norm
    attn_grads = (
        lax.psum_scatter(
            grad_attn_gain.astype(jnp.bfloat16), "fsdp", scatter_dimension=0, tiled=True
        ).astype(jnp.float32),
        lax.psum_scatter(
            grad_query_w.astype(jnp.bfloat16), "fsdp", scatter_dimension=0, tiled=True
        ).astype(jnp.float32),
        lax.psum_scatter(
            grad_key_w.astype(jnp.bfloat16), "fsdp", scatter_dimension=0, tiled=True
        ).astype(jnp.float32),
        lax.psum_scatter(
            grad_value_w.astype(jnp.bfloat16), "fsdp", scatter_dimension=0, tiled=True
        ).astype(jnp.float32),
        lax.psum_scatter(
            grad_out_w.astype(jnp.bfloat16), "fsdp", scatter_dimension=1, tiled=True
        ).astype(jnp.float32),
    )
    attn_grads = (
        lax.psum(attn_grads[0].astype(jnp.bfloat16), "ctx").astype(jnp.float32),
        lax.psum(attn_grads[1].astype(jnp.bfloat16), "ctx").astype(jnp.float32),
        lax.psum(attn_grads[2].astype(jnp.bfloat16), "ctx").astype(jnp.float32),
        lax.psum(attn_grads[3].astype(jnp.bfloat16), "ctx").astype(jnp.float32),
        lax.psum(attn_grads[4].astype(jnp.bfloat16), "ctx").astype(jnp.float32),
    )
    return (
        hidden_out[None],
        input_grad[None],
        attn_grads[0],
        attn_grads[1],
        attn_grads[2],
        attn_grads[3],
        attn_grads[4],
        feed_grads[0],
        feed_grads[1],
        feed_grads[2],
        feed_grads[3],
    )


def solution(mesh):
    placed = (
        P("fsdp", "ctx", None),
        P("fsdp", "ctx"),
        P("fsdp", "ctx", None),
        P("fsdp"),
        P("fsdp", None),
        P("fsdp", None),
        P("fsdp", None),
        P(None, "fsdp"),
        P("fsdp"),
        P(None, "fsdp"),
        P(None, "fsdp"),
        P("fsdp", None),
    )
    return jax.shard_map(
        on_device,
        mesh=mesh,
        in_specs=placed,
        out_specs=(
            P("fsdp", "ctx", None),
            P("fsdp", "ctx", None),
            P("fsdp"),
            P("fsdp", None),
            P("fsdp", None),
            P("fsdp", None),
            P(None, "fsdp"),
            P("fsdp"),
            P(None, "fsdp"),
            P(None, "fsdp"),
            P("fsdp", None),
        ),
        check_vma=False,
    )
```

profile of v0, /device:TPU:0, one launch (start us, length us, event | category | flops | bytes accessed | tf_op | source)
XLA Modules:
  0.0 864.6 jit_solution(7573931468354807353)
XLA Ops:
  21.8 21.9 %all-reduce.7 = (bf16[576]{0:T(1024)(128)(2,1)S(1)}, bf16[576]{0:T(1024)(128)(2,1)S(1)}) all-reduce(bf16[576]{0:T(1024)(128)(2,1)S(1)} %dynamic-update-slice, bf16[576]{0:T(1024)(128)(2,1)S(1)} %dynamic-update-slice.1), channel_id=1, replica_groups=mesh['ctx'=4,'fsdp'=8] {'fsdp'}, use_global_device_ids=true, to_apply=%add | all-reduce | flops 1152 | bytes 4608
  45.0 31.5 %all_gather.40 = bf16[576,192]{1,0:T(8,128)(2,1)S(1)} all-gather(bf16[72,192]{1,0:T(8,128)(2,1)} %param.29), channel_id=1, replica_groups=mesh['ctx'=4,'fsdp'=8] {'fsdp'}, dimensions={0}, use_global_device_ids=true | all-gather | bytes 248832 | tf_op jit(solution)/shard_map/all_gather | solution.py:75
  78.3 35.2 %all_gather.43 = bf16[576,576]{1,0:T(8,128)(2,1)} all-gather(bf16[72,576]{1,0:T(8,128)(2,1)S(1)} %copy-done.34), channel_id=1, replica_groups=mesh['ctx'=4,'fsdp'=8] {'fsdp'}, dimensions={0}, use_global_device_ids=true | all-gather | bytes 746496 | tf_op jit(solution)/shard_map/all_gather | solution.py:74
  118.6 31.3 %all_gather.41 = bf16[576,192]{1,0:T(8,128)(2,1)S(1)} all-gather(bf16[72,192]{1,0:T(8,128)(2,1)S(1)} %copy-done.38), channel_id=1, replica_groups=mesh['ctx'=4,'fsdp'=8] {'fsdp'}, dimensions={0}, use_global_device_ids=true | all-gather | bytes 248832 | tf_op jit(solution)/shard_map/all_gather | solution.py:76
  153.5 12.5 %while.148 = (s32[]{:T(128)}, f32[3,3,512]{2,1,0:T(4,128)}, f32[3,3,512]{2,1,0:T(4,128)}, f32[3,3,512,64]{2,3,1,0:T(8,128)S(1)}, s32[512]{0:T(512)S(1)}, /*index...) while((s32[]{:T(128)}, f32[3,3,512]{2,1,0:T(4,128)}, ...), condition=%wide.region_4.5_spmd, body=%wide.region_1.4_spmd.sunk | while | flops 210345472 | bytes 11295333 | solution.py:133
  169.6 77.1 %while.150 = (s32[]{:T(128)}, bf16[512,384]{0,1:T(8,128)(2,1)}, f32[3,3,512]{2,1,0:T(4,128)}, f32[3,3,512]{2,1,0:T(4,128)}, f32[3,3,512,64]{2,3,1,0:T(8,128)S(1)...) while((s32[]{:T(128)}, bf16[512,384]{0,1:T(8,128)(2,1)}, ...), condition=%wide.region_10.11_spmd, body=%wide.region_5.10_spmd.sunk | while | flops 210442256 | bytes 15647789 | solution.py:230
  177.7 16.8 %while.154 = (s32[]{:T(128)}, f32[3,3,512]{2,1,0:T(4,128)}, f32[3,3,512]{2,1,0:T(4,128)}, f32[3,3,512,64]{2,3,1,0:T(8,128)S(1)}, s32[512]{0:T(512)S(1)}, /*index...) while((s32[]{:T(128)}, f32[3,3,512]{2,1,0:T(4,128)}, ...), condition=%wide.region_9.9_spmd.clone, body=%wide.region_6.8_spmd.clone.sunk | while | flops 210442240 | bytes 12497517 | solution.py:133
  203.4 16.8 %while.154 = (s32[]{:T(128)}, f32[3,3,512]{2,1,0:T(4,128)}, f32[3,3,512]{2,1,0:T(4,128)}, f32[3,3,512,64]{2,3,1,0:T(8,128)S(1)}, s32[512]{0:T(512)S(1)}, /*index...) while((s32[]{:T(128)}, f32[3,3,512]{2,1,0:T(4,128)}, ...), condition=%wide.region_9.9_spmd.clone, body=%wide.region_6.8_spmd.clone.sunk | while | flops 210442240 | bytes 12497517 | solution.py:133
  229.1 16.8 %while.154 = (s32[]{:T(128)}, f32[3,3,512]{2,1,0:T(4,128)}, f32[3,3,512]{2,1,0:T(4,128)}, f32[3,3,512,64]{2,3,1,0:T(8,128)S(1)}, s32[512]{0:T(512)S(1)}, /*index...) while((s32[]{:T(128)}, f32[3,3,512]{2,1,0:T(4,128)}, ...), condition=%wide.region_9.9_spmd.clone, body=%wide.region_6.8_spmd.clone.sunk | while | flops 210442240 | bytes 12497517 | solution.py:133
  247.7 32.1 %all_gather.44 = bf16[576,576]{0,1:T(8,128)(2,1)S(1)} all-gather(bf16[576,72]{0,1:T(8,128)(2,1)S(1)} %copy-done.35), channel_id=1, replica_groups=mesh['ctx'=4,'fsdp'=8] {'fsdp'}, dimensions={1}, use_global_device_ids=true | all-gather | bytes 746496 | tf_op jit(solution)/shard_map/all_gather | solution.py:77
  313.3 20.1 %while.151 = (s32[]{:T(128)}, f32[3,512,3,64]{1,3,2,0:T(8,128)S(1)}, bf16[3,512,64]{1,2,0:T(8,128)(2,1)S(1)}, bf16[3,512,64]{1,2,0:T(8,128)(2,1)S(1)}, bf16[3,51...) while((s32[]{:T(128)}, f32[3,512,3,64]{1,3,2,0:T(8,128)S(1)}, ...), condition=%wide.region_15.16_spmd, body=%wide.region_14.15_spmd.sunk | while | flops 512229376 | bytes 16635009 | solution.py:175
  334.2 89.7 %while.153 = (s32[]{:T(128)}, bf16[512,384]{0,1:T(8,128)(2,1)}, bf16[512,384]{0,1:T(8,128)(2,1)}, f32[3,512,3,64]{1,3,2,0:T(8,128)S(1)}, s32[]{:T(128)}, /*index...) while((s32[]{:T(128)}, bf16[512,384]{0,1:T(8,128)(2,1)}, ...), condition=%wide.region_19.20_spmd, body=%wide.region_16.19_spmd.sunk | while | flops 513114144 | bytes 24110740 | solution.py:257
  342.3 20.2 %while.155 = (s32[]{:T(128)}, f32[3,512,3,64]{1,3,2,0:T(8,128)S(1)}, f32[3,512,64]{1,2,0:T(8,128)S(1)}, f32[3,512,64]{1,2,0:T(8,128)S(1)}, bf16[3,512,64]{1,2,0:...) while((s32[]{:T(128)}, f32[3,512,3,64]{1,3,2,0:T(8,128)S(1)}, ...), condition=%wide.region_18.18_spmd.clone, body=%wide.region_17.17_spmd.clone.sunk | while | flops 512327680 | bytes 17814660 | solution.py:175
  372.2 20.2 %while.155 = (s32[]{:T(128)}, f32[3,512,3,64]{1,3,2,0:T(8,128)S(1)}, f32[3,512,64]{1,2,0:T(8,128)S(1)}, f32[3,512,64]{1,2,0:T(8,128)S(1)}, bf16[3,512,64]{1,2,0:...) while((s32[]{:T(128)}, f32[3,512,3,64]{1,3,2,0:T(8,128)S(1)}, ...), condition=%wide.region_18.18_spmd.clone, body=%wide.region_17.17_spmd.clone.sunk | while | flops 512327680 | bytes 17814660 | solution.py:175
  402.1 20.1 %while.155 = (s32[]{:T(128)}, f32[3,512,3,64]{1,3,2,0:T(8,128)S(1)}, f32[3,512,64]{1,2,0:T(8,128)S(1)}, f32[3,512,64]{1,2,0:T(8,128)S(1)}, bf16[3,512,64]{1,2,0:...) while((s32[]{:T(128)}, f32[3,512,3,64]{1,3,2,0:T(8,128)S(1)}, ...), condition=%wide.region_18.18_spmd.clone, body=%wide.region_17.17_spmd.clone.sunk | while | flops 512327680 | bytes 17814660 | solution.py:175
  454.9 28.8 %reduce-scatter.22.cloned.1.call-done = bf16[72,576]{1,0:T(8,128)(2,1)} async-done(((bf16[576,576]{1,0:T(8,128)(2,1)}), bf16[72,576]{1,0:T(8,128)(2,1)}) %reduce-scatter.22.cloned.1.call-update) | async-done | bytes 82960
  483.7 69.1 %reduce-scatter.16.cloned.1.call-done = bf16[576,192]{0,1:T(8,128)(2,1)} async-done(((bf16[576,1536]{0,1:T(8,128)(2,1)}), bf16[576,192]{0,1:T(8,128)(2,1)}) %reduce-scatter.16.cloned.1.call-update) | async-done | bytes 221200 | tf_op jit(solution)/shard_map/reduce_scatter | solution.py:370
  552.8 69.5 %reduce-scatter.18.cloned.1.call-done = bf16[576,192]{0,1:T(8,128)(2,1)} async-done(((bf16[576,1536]{0,1:T(8,128)(2,1)}), bf16[576,192]{0,1:T(8,128)(2,1)}) %reduce-scatter.18.cloned.1.call-update) | async-done | bytes 221200 | tf_op jit(solution)/shard_map/reduce_scatter | solution.py:373
  622.2 69.2 %reduce-scatter.20.cloned.1.call-done = bf16[192,576]{1,0:T(8,128)(2,1)} async-done(((bf16[1536,576]{1,0:T(8,128)(2,1)}), bf16[192,576]{1,0:T(8,128)(2,1)}) %reduce-scatter.20.cloned.1.call-update) | async-done | bytes 221200 | tf_op jit(solution)/shard_map/reduce_scatter | solution.py:376
  691.5 19.1 %all-reduce.6 = (bf16[576]{0:T(1024)(128)(2,1)S(1)}, bf16[576]{0:T(1024)(128)(2,1)S(1)}) all-reduce(bf16[576]{0:T(1024)(128)(2,1)S(1)} %get-tuple-element.827, bf16[576]{0:T(1024)(128)(2,1)S(1)} %copy-done.43), channel_id=3, replica_groups=mesh['ctx'=4,'fsdp'=8] {'fsdp'}, use_global_device_ids=true, to_apply=%region_22.23.clone | all-reduce | flops 1152 | bytes 4608
  712.1 41.3 %reduce-scatter.12.cloned.1.call-done = bf16[72,192]{1,0:T(8,128)(2,1)} async-done(((bf16[576,192]{1,0:T(8,128)(2,1)}), bf16[72,192]{1,0:T(8,128)(2,1)}) %reduce-scatter.12.cloned.1.call-update) | async-done | bytes 27664 | tf_op jit(solution)/shard_map/reduce_scatter | solution.py:468
  753.3 61.3 %reduce-scatter.14.cloned.1.call-done = bf16[72,192]{1,0:T(8,128)(2,1)} async-done(((bf16[576,192]{1,0:T(8,128)(2,1)}), bf16[72,192]{1,0:T(8,128)(2,1)}) %reduce-scatter.14.cloned.1.call-update) | async-done | bytes 27664 | tf_op jit(solution)/shard_map/reduce_scatter | solution.py:471
  814.6 12.2 %all-reduce.8 = (bf16[72]{0:T(256)(128)(2,1)S(1)}, bf16[72,192]{1,0:T(8,128)(2,1)S(1)}, bf16[72,192]{1,0:T(8,128)(2,1)S(1)}, bf16[72]{0:T(256)(128)(2,1)S(1)}) all-reduce(bf16[72]{0:T(256)(128)(2,1)S(1)} %dynamic-slice.4, bf16[72,192]{1,0:T(8,128)(2,1)} %reduce-scatter.12.cloned.1.call-done, ...), channel_id=1, replica_groups=mesh['ctx'=4,'fsdp'=8] {'ctx'}, use_global_device_ids=true, to_apply=%region_23.24 | all-reduce | flops 27792 | bytes 111168 | tf_op jit(solution)/shard_map/psum | solution.py:479
  829.1 23.2 %all-reduce.12.cloned.1.call-done = (bf16[72,576]{1,0:T(8,128)(2,1)}, bf16[576,72]{0,1:T(8,128)(2,1)}, bf16[576,192]{0,1:T(8,128)(2,1)}, bf16[576,192]{0,1:T(8,128)(2,1)}, bf16[192,576]{1,0:T(8,128)(2,1)}) async-done(((bf16[72,576]{1,0:T(8,128)(2,1)}, bf16[576,72]{0,1:T(8,128)(2,1)}, bf16[576,192]{0,1:T(8,128)(2,1)}, bf16[576,192]{0,1:T(8,128)(2,1)}, bf16[192,576]{1,0:T(8,128)(2,1)}), ...) | async-done | bytes 829456 | tf_op jit(solution)/shard_map/psum | solution.py:480
  (417 shorter events, 302.2 us)
Async XLA Ops:
  7.2 275.7 %all-gather.5.cloned.1.call-start = ((), (), s32[]{:S(2)}) async-start(), calls=%async_computation.7 | async-start | bytes 2211840 | tf_op jit(solution)/shard_map/all_gather | solution.py:84
  7.9 279.8 %all-gather.7.cloned.1.call-start = ((), (), s32[]{:S(2)}) async-start(), calls=%async_computation.8 | async-start | bytes 2211840 | tf_op jit(solution)/shard_map/all_gather | solution.py:85
  8.7 284.0 %all-gather.9.cloned.1.call-start = ((), (), s32[]{:S(2)}) async-start(), calls=%async_computation.9 | async-start | bytes 2211840 | tf_op jit(solution)/shard_map/all_gather | solution.py:86
  9.4 445.5 %reduce-scatter.24.cloned.1.call-start = ((), (), s32[]{:S(2)}) async-start(), calls=%async_computation.16 | async-start | bytes 829440
  43.8 106.2 %copy-start.39 = (f32[576]{0:T(1024)}, f32[576]{0:T(1024)S(1)}, u32[]{:S(2)}) copy-start(f32[576]{0:T(1024)S(1)} %convert_element_type.226) | copy-start | bytes 6916
  169.6 7.4 collective-permute-start.2
  195.3 7.4 collective-permute-start.2
  221.0 7.4 collective-permute-start.2
  311.0 172.7 %reduce-scatter.22.cloned.1.call-start = ((), (), s32[]{:S(2)}) async-start(), calls=%async_computation.15 | async-start | bytes 829440
  334.2 7.4 collective-permute-start
  334.2 29.0 %collective-permute-start.1 = (bf16[512,384]{0,1:T(8,128)(2,1)}, bf16[512,384]{0,1:T(8,128)(2,1)S(1)}, u32[]{:S(2)}, u32[]{:S(2)}) collective-permute-start(bf16[512,384]{0,1:T(8,128)(2,1)} %get-tuple-element.1687), channel_id=1, source_target_pairs={{0,8},{8,16},{16,24},{24,0},{1,9},{9,17},{17,25},{25,1},{2,10},{10... | collective-permute-start | bytes 1179656 | tf_op jit(solution)/shard_map/while/body/eval_jaxpr/ppermute | solution.py:21
  364.1 7.4 collective-permute-start
  364.1 29.0 %collective-permute-start.1 = (bf16[512,384]{0,1:T(8,128)(2,1)}, bf16[512,384]{0,1:T(8,128)(2,1)S(1)}, u32[]{:S(2)}, u32[]{:S(2)}) collective-permute-start(bf16[512,384]{0,1:T(8,128)(2,1)} %get-tuple-element.1687), channel_id=1, source_target_pairs={{0,8},{8,16},{16,24},{24,0},{1,9},{9,17},{17,25},{25,1},{2,10},{10... | collective-permute-start | bytes 1179656 | tf_op jit(solution)/shard_map/while/body/eval_jaxpr/ppermute | solution.py:21
  394.0 7.4 collective-permute-start
  394.0 29.0 %collective-permute-start.1 = (bf16[512,384]{0,1:T(8,128)(2,1)}, bf16[512,384]{0,1:T(8,128)(2,1)S(1)}, u32[]{:S(2)}, u32[]{:S(2)}) collective-permute-start(bf16[512,384]{0,1:T(8,128)(2,1)} %get-tuple-element.1687), channel_id=1, source_target_pairs={{0,8},{8,16},{16,24},{24,0},{1,9},{9,17},{17,25},{25,1},{2,10},{10... | collective-permute-start | bytes 1179656 | tf_op jit(solution)/shard_map/while/body/eval_jaxpr/ppermute | solution.py:21
  426.7 126.1 %reduce-scatter.16.cloned.1.call-start = ((), (), s32[]{:S(2)}) async-start(), calls=%async_computation.12 | async-start | bytes 2211840 | tf_op jit(solution)/shard_map/reduce_scatter | solution.py:370
  431.0 191.3 %reduce-scatter.18.cloned.1.call-start = ((), (), s32[]{:S(2)}) async-start(), calls=%async_computation.13 | async-start | bytes 2211840 | tf_op jit(solution)/shard_map/reduce_scatter | solution.py:373
  435.2 256.2 %reduce-scatter.20.cloned.1.call-start = ((), (), s32[]{:S(2)}) async-start(), calls=%async_computation.14 | async-start | bytes 2211840 | tf_op jit(solution)/shard_map/reduce_scatter | solution.py:376
  440.4 312.9 %reduce-scatter.12.cloned.1.call-start = ((), (), s32[]{:S(2)}) async-start(), calls=%async_computation.10 | async-start | bytes 331776 | tf_op jit(solution)/shard_map/reduce_scatter | solution.py:468
  441.4 7.5 collective-permute-start.3
  450.2 364.4 %reduce-scatter.14.cloned.1.call-start = ((), (), s32[]{:S(2)}) async-start(), calls=%async_computation.11 | async-start | bytes 331776 | tf_op jit(solution)/shard_map/reduce_scatter | solution.py:471
  452.3 400.0 %all-reduce.12.cloned.1.call-start = ((), (), s32[]{:S(2)}) async-start(), calls=%async_computation.17 | async-start | bytes 1843200 | tf_op jit(solution)/shard_map/psum | solution.py:480
  453.3 238.2 %copy-start.43 = (bf16[576]{0:T(1024)(128)(2,1)S(1)}, bf16[576]{0:T(1024)(128)(2,1)}, u32[]{:S(2)}) copy-start(bf16[576]{0:T(1024)(128)(2,1)} %get-tuple-element.825) | copy-start | bytes 3460
  453.3 257.5 %copy-start.3 = (f32[512,576]{0,1:T(8,128)S(1)}, f32[512,576]{0,1:T(8,128)}, u32[]{:S(2)}) copy-start(f32[512,576]{0,1:T(8,128)} %copy-done.2) | copy-start | bytes 3538948
  (43 other events, 502.8 us)
Sparse Core Ops, SparseCore 0:
  10.2 53.8 all-gather.4
  66.3 52.3 all-gather.6
  120.9 46.7 all-gather.8
  311.1 56.9 reduce-scatter.23
  426.8 56.8 reduce-scatter.21
  487.1 65.6 reduce-scatter.15
  556.7 65.5 reduce-scatter.17
  625.7 65.6 reduce-scatter.19
  695.6 57.6 reduce-scatter.11
  756.8 57.7 reduce-scatter.13
  817.6 34.7 all-reduce.11
where the time goes:
time: 868 us; the launch traced here: 865 us
  waiting for transfers between devices  405 us (47%)
  blocking collectives  191 us (22%)
  matrix products  151 us (17%)
  other arithmetic  60.6 us (7%)
  local copies, waits for them, and re-layouts  36.2 us (4%)
  between operations  15.7 us (2%)
    reduce_scatter x1, waiting for transfers between devices, on_device(): lax.psum_scatter(grad_up_w.astype(jnp.bfloat16), 'fsdp', scatter_dimensio...  69.5 us
    reduce_scatter x1, waiting for transfers between devices, on_device(): lax.psum_scatter(grad_down_w.astype(jnp.bfloat16), 'fsdp', scatter_dimens...  69.2 us
    reduce_scatter x1, waiting for transfers between devices, on_device(): lax.psum_scatter(grad_gate_w.astype(jnp.bfloat16), 'fsdp', scatter_dimens...  69.1 us
    reduce_scatter x1, waiting for transfers between devices, on_device(): lax.psum_scatter(grad_value_w.astype(jnp.bfloat16), 'fsdp', scatter_dimen...  61.3 us
    reduce_scatter x1, waiting for transfers between devices, on_device(): lax.psum_scatter(grad_key_w.astype(jnp.bfloat16), 'fsdp', scatter_dimensi...  41.3 us
    unnamed x2, blocking collectives  41.1 us
    ppermute x10, waiting for transfers between devices, from_behind(): return lax.ppermute(value, axis, pairs)  40.9 us
    all_gather x1, blocking collectives, attention_weights(): lax.all_gather(query_weight, 'fsdp', axis=0, tiled=True)  35.2 us
  transfers between devices with their start and end apart: 21, of which 14 were waited for; matrix products, arithmetic and copies ran while one was open for 26% of the time, Pallas kernels for 0%

commit v1 on v0

v1 whole, which is shorter than its diff:
```python
import functools
import math

import jax
import jax.numpy as jnp
from jax import lax
from jax.experimental import pallas as pl
from jax.experimental.pallas import tpu as pltpu
from jax.sharding import PartitionSpec as P

QUERY_HEADS = 9
KEY_VALUE_HEADS = 3
HEAD_FEATURES = 64
GROUP = QUERY_HEADS // KEY_VALUE_HEADS
HALF = HEAD_FEATURES // 2
RUN = 256
QUERY_WIDTH = QUERY_HEADS * HEAD_FEATURES
KV_WIDTH = 2 * KEY_VALUE_HEADS * HEAD_FEATURES
PROJECTED = QUERY_WIDTH + KV_WIDTH
PADDED = 1024
SCALE = 1.0 / math.sqrt(HEAD_FEATURES)

rms_epsilon = 1e-05
rope_base = 100000.0
score_after_mask = -1e30
bf16 = jnp.bfloat16
f32 = jnp.float32
VMEM_BYTES = 60 * 1024 * 1024


def dot(left, right, left_dim, right_dim):
    return lax.dot_general(
        left, right, (((left_dim,), (right_dim,)), ((), ())), preferred_element_type=f32
    )


def swap(value, axis, bit):
    count = lax.axis_size(axis)
    return lax.ppermute(value, axis, [(source, source ^ bit) for source in range(count)])


def axis_bits(axis):
    count = lax.axis_size(axis)
    return [1 << place for place in range(count.bit_length() - 1)]


def gather_slots(value, axis, bits):
    stack = value[None]
    labels = [0]
    for bit in bits:
        stack = jnp.concatenate([stack, swap(stack, axis, bit)], axis=0)
        labels = labels + [label ^ bit for label in labels]
    return stack, tuple(labels)


def add_low(left, right):
    return (left.astype(f32) + right.astype(f32)).astype(bf16)


def scatter_slots(stack, axis, bits):
    for bit in reversed(bits):
        half = stack.shape[0] // 2
        stack = add_low(stack[:half], swap(stack[half:], axis, bit))
    return stack[0]


def rotate(rows, cosine, sine):
    first, second = rows[:HALF], rows[HALF:]
    return jnp.concatenate([first * cosine - second * sine, second * cosine + first * sine], axis=0)


def rotate_back(rows, cosine, sine):
    first, second = rows[:HALF], rows[HALF:]
    return jnp.concatenate([first * cosine + second * sine, second * cosine - first * sine], axis=0)


def run_slice(run):
    return pl.ds(pl.multiple_of(run * RUN, RUN), RUN)


def project_kernel(
    labels, info, hidden, w_own, w_pair, cosine, sine,
    query_t, kv_t, kv_rows, normed_out, weight_t, gains, pieces,
):
    step = pl.program_id(0)
    width = hidden.shape[2] - HEAD_FEATURES
    tokens = hidden.shape[1]
    shards = len(labels)

    @pl.when(step == 0)
    def _():
        me, core = info[0], info[1]
        for slot, label in enumerate(labels):
            pieces[core, me ^ label] = w_own[slot]
            pieces[1 - core, me ^ label] = w_pair[slot]
        part = PADDED // 2
        for side in range(2):
            whole = jnp.concatenate([pieces[side, s].astype(f32) for s in range(shards)], axis=0)
            turned = whole.T
            weight_t[side * part : (side + 1) * part, :] = turned.astype(bf16)
            if side == 1:
                gains[...] = turned[PROJECTED - part : PROJECTED - part + 8]

    rows = hidden[0, :, :width].astype(f32)
    scale = lax.rsqrt(jnp.mean(rows * rows, axis=-1, keepdims=True) + rms_epsilon)
    normed = (rows * scale * gains[0:1, :]).astype(bf16)
    normed_out[0] = normed
    kv = dot(weight_t[QUERY_WIDTH:PROJECTED, :], normed, 1, 1)
    pair = 2 * HEAD_FEATURES
    per_slot = tokens // RUN
    for j in range(per_slot):
        run = info[2 + step * per_slot + j]
        cos, sin = cosine[:, run_slice(run)], sine[:, run_slice(run)]
        columns = slice(j * RUN, (j + 1) * RUN)
        for g in range(KEY_VALUE_HEADS):
            block = kv[g * pair : (g + 1) * pair, columns]
            block = jnp.concatenate(
                [rotate(block[:HEAD_FEATURES], cos, sin), block[HEAD_FEATURES:]], axis=0
            )
            kv_t[g * pair : (g + 1) * pair, columns] = block.astype(bf16)
            kv_rows[g, columns, :] = block.T.astype(bf16)

    @pl.when(step == 0)
    def _():
        queries = dot(weight_t[:QUERY_WIDTH, :], normed, 1, 1)
        for j in range(per_slot):
            run = info[2 + j]
            cos, sin = cosine[:, run_slice(run)], sine[:, run_slice(run)]
            columns = slice(j * RUN, (j + 1) * RUN)
            for h in range(QUERY_HEADS):
                lines = slice(h * HEAD_FEATURES, (h + 1) * HEAD_FEATURES)
                query_t[lines, columns] = (
                    rotate(queries[lines, columns], cos, sin) * SCALE
                ).astype(bf16)


def side_by_side(ref, j):
    return jnp.concatenate(
        [
            ref[h * HEAD_FEATURES : (h + 1) * HEAD_FEATURES, j * RUN : (j + 1) * RUN]
            for h in range(GROUP)
        ],
        axis=1,
    )


def causal():
    shape = (RUN, GROUP * RUN)
    keys = lax.broadcasted_iota(jnp.int32, shape, 0)
    queries = lax.broadcasted_iota(jnp.int32, shape, 1) & (RUN - 1)
    return keys <= queries


def attend_kernel(info, query_t, kv_t, kv_rows, attended_t, log_totals, maxima, totals, sums):
    runs = kv_rows.shape[1] // RUN
    for j in range(query_t.shape[1] // RUN):
        query = side_by_side(query_t, j)
        query = jnp.concatenate([query, jnp.zeros_like(query)], axis=0)
        here = slice(j * RUN, (j + 1) * RUN)
        scores = jnp.where(causal(), dot(kv_rows[0, here, :], query, 1, 0), score_after_mask)
        top = jnp.max(scores, axis=0, keepdims=True)
        weights = jnp.exp(scores - top)
        maxima[...] = top
        totals[...] = jnp.sum(weights, axis=0, keepdims=True)
        sums[...] = dot(kv_t[HEAD_FEATURES:, here], weights.astype(bf16), 1, 0)

        def advance(place, nothing):
            @pl.when(info[2 + place] < info[2 + j])
            def _():
                scores = dot(kv_rows[0, run_slice(place), :], query, 1, 0)
                before = maxima[...]
                top = jnp.maximum(before, jnp.max(scores, axis=0, keepdims=True))
                factor = jnp.exp(before - top)
                weights = jnp.exp(scores - top)
                maxima[...] = top
                totals[...] = totals[...] * factor + jnp.sum(weights, axis=0, keepdims=True)
                sums[...] = sums[...] * factor + dot(
                    kv_t[HEAD_FEATURES:, run_slice(place)], weights.astype(bf16), 1, 0
                )

            return nothing

        lax.fori_loop(0, runs, advance, 0)
        result = sums[...] / totals[...]
        logs = maxima[...] + jnp.log(totals[...])
        for h in range(GROUP):
            columns = slice(h * RUN, (h + 1) * RUN)
            attended_t[h * HEAD_FEATURES : (h + 1) * HEAD_FEATURES, here] = result[:, columns]
            log_totals[0, h : h + 1, here] = logs[:, columns]


def middle_kernel(
    labels, info, hidden, attended_t, b_own, b_pair, gains, middle_out, normed_out, out_weight, pieces
):
    me, core = info[0], info[1]
    half = pieces.shape[2]
    first = b_own.shape[1] - half
    shards = len(labels)
    width = hidden.shape[1]
    shard_rows = width // shards
    for slot, label in enumerate(labels):
        pieces[core, me ^ label] = b_own[slot, first:, :]
        pieces[1 - core, me ^ label] = b_pair[slot, first:, :]
    parts = []
    for s in range(shards):
        parts.append(pieces[0, s].astype(f32)[: min(half, shard_rows)])
        if shard_rows > half:
            parts.append(pieces[1, s].astype(f32)[: shard_rows - half])
    weight = jnp.concatenate(parts, axis=0).T.astype(bf16)
    out_weight[...] = weight
    attended = attended_t[...].astype(bf16)
    middle = hidden[...].astype(f32) + dot(attended, weight, 0, 0)
    scale = lax.rsqrt(jnp.mean(middle * middle, axis=-1, keepdims=True) + rms_epsilon)
    middle_out[...] = middle
    normed_out[...] = (middle * scale * gains[1:2, :]).astype(bf16)


def feed_kernel(
    labels, info, normed, out_grad, middle_in, out_weight, gains, attended_t,
    a_own, a_pair, b_own, b_pair,
    hidden_out, grad_middle_out, grad_att_t, deltas, ga_own, ga_pair, gb_own, gb_pair, gain_grad,
    total, back, pieces,
):
    me, core = info[0], info[1]
    shards = len(labels)
    width = normed.shape[1]
    half = pieces.shape[1] // 2
    total[...] = middle_in[...]
    back[...] = jnp.zeros_like(back)
    for source, target, unit in (
        (a_own, ga_own, a_own.shape[1] // 3),
        (a_pair, ga_pair, a_own.shape[1] // 3),
        (b_own, gb_own, (b_own.shape[1] - half) // 3),
        (b_pair, gb_pair, (b_own.shape[1] - half) // 3),
    ):
        lines = shards * unit
        gate_w = source[:, :unit, :].reshape(lines, width)
        up_w = source[:, unit : 2 * unit, :].reshape(lines, width)
        down_w = source[:, 2 * unit : 3 * unit, :].reshape(lines, width)
        gate = dot(normed[...], gate_w, 1, 1)
        up = dot(normed[...], up_w, 1, 1)
        sigmoid = jax.nn.sigmoid(gate)
        silu = gate * sigmoid
        activated = (silu * up).astype(bf16)
        total[...] += dot(activated, down_w, 1, 0)
        grad_act = dot(out_grad[...], down_w, 1, 1)
        grad_gate = (grad_act * up * sigmoid * (1.0 + gate * (1.0 - sigmoid))).astype(bf16)
        grad_up = (grad_act * silu).astype(bf16)
        back[...] += dot(grad_gate, gate_w, 1, 0) + dot(grad_up, up_w, 1, 0)
        target[:, :unit, :] = dot(grad_gate, normed[...], 0, 0).astype(bf16).reshape(shards, unit, width)
        target[:, unit : 2 * unit, :] = (
            dot(grad_up, normed[...], 0, 0).astype(bf16).reshape(shards, unit, width)
        )
        target[:, 2 * unit : 3 * unit, :] = (
            dot(activated, out_grad[...], 0, 0).astype(bf16).reshape(shards, unit, width)
        )
    hidden_out[...] = total[...].astype(bf16)
    middle = middle_in[...]
    scale = lax.rsqrt(jnp.mean(middle * middle, axis=-1, keepdims=True) + rms_epsilon)
    unit_rows = middle * scale
    grad_normed = back[...]
    grad_unit = grad_normed * gains[1:2, :]
    mean = jnp.mean(grad_unit * unit_rows, axis=-1, keepdims=True)
    grad_middle = out_grad[...].astype(f32) + scale * (grad_unit - unit_rows * mean)
    grad_middle_out[...] = grad_middle
    gain_grad[...] = jnp.concatenate(
        [jnp.sum(grad_normed * unit_rows, axis=0, keepdims=True), jnp.zeros((7, width), f32)], axis=0
    )
    low = grad_middle.astype(bf16)
    grad_att = dot(out_weight[...], low, 1, 1).astype(bf16)
    grad_att_t[...] = grad_att
    for h in range(QUERY_HEADS):
        lines = slice(h * HEAD_FEATURES, (h + 1) * HEAD_FEATURES)
        deltas[h // GROUP, h % GROUP : h % GROUP + 1, :] = jnp.sum(
            grad_att[lines].astype(f32) * attended_t[lines, :], axis=0, keepdims=True
        )
    grad_weight = dot(attended_t[...].astype(bf16), low, 1, 0).T
    shard_rows = width // shards
    pieces[...] = jnp.zeros_like(pieces)
    for s in range(shards):
        pieces[s, :shard_rows, :] = grad_weight[s * shard_rows : (s + 1) * shard_rows]
    first = b_own.shape[1] - half
    for slot, label in enumerate(labels):
        for target, side in ((gb_own, core), (gb_pair, 1 - core)):
            lines = pl.ds(pl.multiple_of(side * half, 16), half)
            target[slot, first:, :] = pieces[me ^ label, lines, :].astype(bf16)


def attend_back_kernel(
    info, query_t, kv_t, kv_rows, grad_att_t, log_totals, deltas, cosine, sine,
    grad_query_t, grad_kv_t, kv_sums, query_sums,
):
    runs = kv_rows.shape[1] // RUN
    own = query_t.shape[1] // RUN
    kv_sums[...] = jnp.zeros_like(kv_sums)
    for j in range(own):
        query = side_by_side(query_t, j)
        grad = side_by_side(grad_att_t, j)
        empty = jnp.zeros_like(query)
        query_deep = jnp.concatenate([query, empty], axis=0)
        grad_deep = jnp.concatenate([empty, grad], axis=0)
        query_rows = query_deep.T
        grad_rows = grad_deep.T
        here = slice(j * RUN, (j + 1) * RUN)
        logs = jnp.concatenate([log_totals[0, h : h + 1, here] for h in range(GROUP)], axis=1)
        delta = jnp.concatenate([deltas[0, h : h + 1, here] for h in range(GROUP)], axis=1)

        def tile(place, masked):
            kv = kv_rows[0, place, :]
            probabilities = jnp.exp(dot(kv, query_deep, 1, 0) - logs)
            if masked:
                probabilities = jnp.where(causal(), probabilities, 0.0)
            grad_scores = probabilities * (dot(kv, grad_deep, 1, 0) - delta)
            low = grad_scores.astype(bf16)
            kv_sums[place, :] += dot(low, query_rows, 1, 0) + dot(
                probabilities.astype(bf16), grad_rows, 1, 0
            )
            return dot(kv_t[:HEAD_FEATURES, place], low, 1, 0)

        query_sums[...] = tile(here, True)

        def advance(place, nothing):
            @pl.when(info[2 + place] < info[2 + j])
            def _():
                query_sums[...] += tile(run_slice(place), False)

            return nothing

        lax.fori_loop(0, runs, advance, 0)
        run = info[2 + j]
        cos, sin = cosine[:, run_slice(run)], sine[:, run_slice(run)]
        for h in range(GROUP):
            part = query_sums[:, h * RUN : (h + 1) * RUN] * SCALE
            grad_query_t[h * HEAD_FEATURES : (h + 1) * HEAD_FEATURES, here] = rotate_back(
                part, cos, sin
            ).astype(bf16)

    def turn(slot, nothing):
        for j in range(own):
            place = slot * own + j
            run = info[2 + place]
            cos, sin = cosine[:, run_slice(run)], sine[:, run_slice(run)]
            block = kv_sums[run_slice(place), :].T
            grad_kv_t[slot, 0, :, j * RUN : (j + 1) * RUN] = jnp.concatenate(
                [rotate_back(block[:HEAD_FEATURES], cos, sin), block[HEAD_FEATURES:]], axis=0
            ).astype(bf16)
        return nothing

    lax.fori_loop(0, runs // own, turn, 0)


def weight_grad_kernel(
    labels, info, grad_query_t, grad_kv_t, normed, weight_t, gains, feed_gain, g_own, g_pair, sums, pieces
):
    step = pl.program_id(0)
    width = normed.shape[2]
    shards = len(labels)
    shard_rows = width // shards
    part = PADDED // 2

    @pl.when(step == 0)
    def _():
        sums[:QUERY_WIDTH, :] = dot(grad_query_t[...], normed[0], 1, 0)
        sums[QUERY_WIDTH:, :] = jnp.zeros((PADDED - QUERY_WIDTH, width), f32)

    sums[QUERY_WIDTH:PROJECTED, :] += dot(
        grad_kv_t[0].reshape(KV_WIDTH, grad_kv_t.shape[3]), normed[0], 1, 0
    )

    @pl.when(step == pl.num_programs(0) - 1)
    def _():
        me, core = info[0], info[1]
        products = sums[:PROJECTED, :] * weight_t[:PROJECTED, :].astype(f32)
        sums[PROJECTED : PROJECTED + 1, :] = jnp.sum(products, axis=0, keepdims=True) / gains[0:1, :]
        sums[PROJECTED + 1 : PROJECTED + 2, :] = feed_gain[0:1, :]
        for side in range(2):
            turned = sums[side * part : (side + 1) * part, :].T
            for s in range(shards):
                pieces[side, s] = turned[s * shard_rows : (s + 1) * shard_rows].astype(bf16)
        for slot, label in enumerate(labels):
            g_own[slot] = pieces[core, me ^ label]
            g_pair[slot] = pieces[1 - core, me ^ label]


def input_grad_kernel(grad_query_t, grad_kv_t, weight_t, hidden, grad_middle, gains, input_grad):
    grad_normed = dot(grad_query_t[...], weight_t[:QUERY_WIDTH, :], 0, 0) + dot(
        grad_kv_t[...], weight_t[QUERY_WIDTH:PROJECTED, :], 0, 0
    )
    rows = hidden[...].astype(f32)
    scale = lax.rsqrt(jnp.mean(rows * rows, axis=-1, keepdims=True) + rms_epsilon)
    unit_rows = rows * scale
    grad_unit = grad_normed * gains[0:1, :]
    mean = jnp.mean(grad_unit * unit_rows, axis=-1, keepdims=True)
    input_grad[...] = grad_middle[...] + scale * (grad_unit - unit_rows * mean)


def shape(dims, kind):
    return jax.ShapeDtypeStruct(dims, kind)


SCALARS = pl.BlockSpec(memory_space=pltpu.SMEM)


def whole(array):
    count = len(array.shape)
    return pl.BlockSpec(array.shape, lambda *step: (0,) * count)


def call(kernel, outputs, flops, grid=(), ins=None, outs=None, scratch=()):
    return pl.pallas_call(
        kernel,
        out_shape=outputs,
        grid=grid,
        in_specs=ins,
        out_specs=outs if outs is not None else [whole(o) for o in outputs],
        scratch_shapes=scratch,
        compiler_params=pltpu.CompilerParams(vmem_limit_bytes=VMEM_BYTES),
        cost_estimate=pl.CostEstimate(flops=int(flops), bytes_accessed=0, transcendentals=0),
    )


def on_device(
    hidden_in,
    positions,
    out_grad,
    attn_gain,
    query_weight,
    key_matrix,
    value_matrix,
    out_weight,
    mlp_gain,
    gate_weight,
    up_weight,
    down_weight,
):
    hidden = hidden_in[0]
    tokens, width = hidden.shape
    blocks = lax.axis_size("ctx")
    shards = lax.axis_size("fsdp")
    length = blocks * tokens
    me = lax.axis_index("fsdp")
    ctx = lax.axis_index("ctx")
    core = ctx & 1
    shard_rows = width // shards
    ff_rows = down_weight.shape[0]
    fbits = axis_bits("fsdp")
    high_to_low = tuple(reversed(fbits))
    low_then_high = (fbits[0],) + tuple(reversed(fbits[1:]))
    ctx_bits = axis_bits("ctx")

    run_ids = (positions[0] // RUN).astype(bf16)
    extended = jnp.concatenate(
        [hidden, jnp.broadcast_to(run_ids[:, None], (tokens, HEAD_FEATURES))], axis=1
    )
    gathered = {0: extended}
    for bit in reversed(ctx_bits):
        for label in list(gathered):
            gathered[label ^ bit] = swap(gathered[label], "ctx", bit)
    hidden_all = jnp.stack([gathered[label] for label in range(blocks)])
    runs = hidden_all[:, ::RUN, width].reshape(-1).astype(jnp.int32)
    info = jnp.concatenate([jnp.stack([me, core]).astype(jnp.int32), runs])

    frequencies = rope_base ** (-jnp.arange(HALF, dtype=f32) / HALF)
    angles = frequencies[:, None] * jnp.arange(length, dtype=jnp.int32).astype(f32)[None, :]
    cosine, sine = jnp.cos(angles), jnp.sin(angles)

    pair = (shard_rows, KEY_VALUE_HEADS, HEAD_FEATURES)
    kv_columns = jnp.concatenate(
        [key_matrix.reshape(pair), value_matrix.reshape(pair)], axis=2
    ).reshape(shard_rows, KV_WIDTH)
    projections = jnp.concatenate(
        [
            query_weight,
            kv_columns,
            attn_gain[:, None],
            mlp_gain[:, None],
            jnp.zeros((shard_rows, PADDED - PROJECTED - 2), bf16),
        ],
        axis=1,
    )
    part = PADDED // 2
    w_own, w_labels = gather_slots(
        lax.dynamic_slice_in_dim(projections, core * part, part, axis=1), "fsdp", high_to_low
    )
    w_pair = swap(w_own, "ctx", 1)

    half = -(-shard_rows // 32) * 16
    unit_a, unit_b = ff_rows // 3, ff_rows // 6
    feed = jnp.stack([gate_weight.T, up_weight.T, down_weight])
    out_rows = jnp.pad(out_weight.T, ((0, 2 * half - shard_rows), (0, 0)))
    mine_a = lax.dynamic_slice_in_dim(feed, core * unit_a, unit_a, axis=1).reshape(3 * unit_a, width)
    mine_b = lax.dynamic_slice_in_dim(feed, 2 * unit_a + core * unit_b, unit_b, axis=1)
    mine_b = jnp.concatenate(
        [
            mine_b.reshape(3 * unit_b, width),
            lax.dynamic_slice_in_dim(out_rows, core * half, half, axis=0),
        ],
        axis=0,
    )
    b_own, b_labels = gather_slots(mine_b, "fsdp", low_then_high)
    b_pair = swap(b_own, "ctx", 1)
    a_own, _ = gather_slots(mine_a, "fsdp", high_to_low)
    a_pair = swap(a_own, "ctx", 1)

    heads_t = shape((QUERY_WIDTH, tokens), bf16)
    per_block = pl.BlockSpec((1, tokens, width), lambda r: (r, 0, 0))
    pair_width = 2 * HEAD_FEATURES
    query_t, kv_t, kv_rows, normed_all, weight_t, gains = call(
        functools.partial(project_kernel, w_labels),
        [
            heads_t,
            shape((KV_WIDTH, length), bf16),
            shape((KEY_VALUE_HEADS, length, pair_width), bf16),
            shape((blocks, tokens, width), bf16),
            shape((PADDED, width), bf16),
            shape((8, width), f32),
        ],
        2 * width * (tokens * QUERY_WIDTH + length * KV_WIDTH),
        grid=(blocks,),
        ins=[
            SCALARS,
            pl.BlockSpec((1, tokens, width + HEAD_FEATURES), lambda r: (r, 0, 0)),
            whole(w_own),
            whole(w_pair),
            whole(cosine),
            whole(sine),
        ],
        outs=[
            whole(heads_t),
            pl.BlockSpec((KV_WIDTH, tokens), lambda r: (0, r)),
            pl.BlockSpec((KEY_VALUE_HEADS, tokens, pair_width), lambda r: (0, r, 0)),
            per_block,
            pl.BlockSpec((PADDED, width), lambda r: (0, 0)),
            pl.BlockSpec((8, width), lambda r: (0, 0)),
        ],
        scratch=[pltpu.VMEM((2, shards, shard_rows, part), bf16)],
    )(info, hidden_all, w_own, w_pair, cosine, sine)

    group_rows = pl.BlockSpec((GROUP * HEAD_FEATURES, tokens), lambda g: (g, 0))
    group_kv_t = pl.BlockSpec((pair_width, length), lambda g: (g, 0))
    group_kv = pl.BlockSpec((1, length, pair_width), lambda g: (g, 0, 0))
    group_line = pl.BlockSpec((1, GROUP, tokens), lambda g: (g, 0, 0))
    lines = shape((KEY_VALUE_HEADS, GROUP, tokens), f32)
    attended_t, log_totals = call(
        attend_kernel,
        [shape((QUERY_WIDTH, tokens), f32), lines],
        4 * 4 * tokens * length * QUERY_WIDTH,
        grid=(KEY_VALUE_HEADS,),
        ins=[SCALARS, group_rows, group_kv_t, group_kv],
        outs=[group_rows, group_line],
        scratch=[
            pltpu.VMEM((1, GROUP * RUN), f32),
            pltpu.VMEM((1, GROUP * RUN), f32),
            pltpu.VMEM((HEAD_FEATURES, GROUP * RUN), f32),
        ],
    )(info, query_t, kv_t, kv_rows)

    low_rows = shape((tokens, width), bf16)
    wide_rows = shape((tokens, width), f32)
    square = shape((QUERY_WIDTH, width), bf16)
    middle, normed_mlp, full_out = call(
        functools.partial(middle_kernel, b_labels),
        [wide_rows, low_rows, square],
        2 * tokens * width * QUERY_WIDTH,
        ins=[SCALARS] + [whole(x) for x in (hidden, attended_t, b_own, b_pair, gains)],
        scratch=[pltpu.VMEM((2, shards, half, width), bf16)],
    )(info, hidden, attended_t, b_own, b_pair, gains)

    feed_ins = (normed_mlp, out_grad[0], middle, full_out, gains, attended_t, a_own, a_pair, b_own, b_pair)
    (
        hidden_out, grad_middle, grad_att_t, deltas, ga_own, ga_pair, gb_own, gb_pair, feed_gain,
    ) = call(
        functools.partial(feed_kernel, b_labels),
        [
            low_rows,
            wide_rows,
            heads_t,
            lines,
            shape(a_own.shape, bf16),
            shape(a_own.shape, bf16),
            shape(b_own.shape, bf16),
            shape(b_own.shape, bf16),
            shape((8, width), f32),
        ],
        18 * tokens * width * ff_rows * shards,
        ins=[SCALARS] + [whole(x) for x in feed_ins],
        scratch=[
            pltpu.VMEM((tokens, width), f32),
            pltpu.VMEM((tokens, width), f32),
            pltpu.VMEM((shards, 2 * half, width), f32),
        ],
    )(info, *feed_ins)

    def settle(own, other, bits):
        stack = add_low(own, swap(other, "ctx", 1))
        value = scatter_slots(stack, "fsdp", bits)
        for bit in ctx_bits[1:]:
            value = add_low(value, swap(value, "ctx", bit))
        other = swap(value, "ctx", 1)
        first = jnp.where(core == 0, value, other)
        second = jnp.where(core == 0, other, value)
        return first.astype(f32), second.astype(f32)

    first_a, second_a = settle(ga_own, ga_pair, high_to_low)
    first_b, second_b = settle(gb_own, gb_pair, low_then_high)
    grads = []
    for place in range(3):
        rows_a = slice(place * unit_a, (place + 1) * unit_a)
        rows_b = slice(place * unit_b, (place + 1) * unit_b)
        grads.append(
            jnp.concatenate([first_a[rows_a], second_a[rows_a], first_b[rows_b], second_b[rows_b]], axis=0)
        )
    out_grad_rows = jnp.concatenate([first_b[3 * unit_b :], second_b[3 * unit_b :]], axis=0)[:shard_rows]

    slots = shape((blocks, KEY_VALUE_HEADS, pair_width, tokens), bf16)
    grad_query_t, grad_kv_t = call(
        attend_back_kernel,
        [heads_t, slots],
        10 * 4 * tokens * length * QUERY_WIDTH,
        grid=(KEY_VALUE_HEADS,),
        ins=[SCALARS, group_rows, group_kv_t, group_kv, group_rows, group_line, group_line]
        + [whole(cosine), whole(sine)],
        outs=[
            group_rows,
            pl.BlockSpec((blocks, 1, pair_width, tokens), lambda g: (0, g, 0, 0)),
        ],
        scratch=[
            pltpu.VMEM((length, pair_width), f32),
            pltpu.VMEM((HEAD_FEATURES, GROUP * RUN), f32),
        ],
    )(info, query_t, kv_t, kv_rows, grad_att_t, log_totals, deltas, cosine, sine)

    own_kv = grad_kv_t
    for bit in ctx_bits:
        pairs = own_kv.reshape((own_kv.shape[0] // 2, 2) + own_kv.shape[1:])
        own_kv = add_low(pairs[:, 0], swap(pairs[:, 1], "ctx", bit))
    own_kv = own_kv.reshape(KV_WIDTH, tokens)

    pieces = shape((shards, shard_rows, part), bf16)
    g_own, g_pair = call(
        functools.partial(weight_grad_kernel, w_labels),
        [pieces, pieces],
        2 * width * (tokens * QUERY_WIDTH + length * KV_WIDTH),
        grid=(blocks,),
        ins=[
            SCALARS,
            whole(heads_t),
            pl.BlockSpec((1, KEY_VALUE_HEADS, pair_width, tokens), lambda r: (r, 0, 0, 0)),
            per_block,
            whole(weight_t),
            whole(gains),
            whole(feed_gain),
        ],
        scratch=[
            pltpu.VMEM((PADDED, width), f32),
            pltpu.VMEM((2, shards, shard_rows, part), bf16),
        ],
    )(info, grad_query_t, grad_kv_t, normed_all, weight_t, gains, feed_gain)
    projection_grads = jnp.concatenate(settle(g_own, g_pair, high_to_low), axis=1)

    last_ins = (grad_query_t, own_kv, weight_t, hidden, grad_middle, gains)
    (input_grad,) = call(
        input_grad_kernel,
        [wide_rows],
        2 * tokens * width * PROJECTED,
        ins=[whole(x) for x in last_ins],
    )(*last_ins)

    kv_grads = projection_grads[:, QUERY_WIDTH:PROJECTED].reshape(shard_rows, KEY_VALUE_HEADS, pair_width)
    return (
        hidden_out[None],
        input_grad[None],
        projection_grads[:, PROJECTED],
        projection_grads[:, :QUERY_WIDTH],
        kv_grads[:, :, :HEAD_FEATURES].reshape(shard_rows, -1),
        kv_grads[:, :, HEAD_FEATURES:].reshape(shard_rows, -1),
        out_grad_rows.T,
        projection_grads[:, PROJECTED + 1],
        grads[0].T,
        grads[1].T,
        grads[2],
    )


def solution(mesh):
    placed = (
        P("fsdp", "ctx", None),
        P("fsdp", "ctx"),
        P("fsdp", "ctx", None),
        P("fsdp"),
        P("fsdp", None),
        P("fsdp", None),
        P("fsdp", None),
        P(None, "fsdp"),
        P("fsdp"),
        P(None, "fsdp"),
        P(None, "fsdp"),
        P("fsdp", None),
    )
    return jax.shard_map(
        on_device,
        mesh=mesh,
        in_specs=placed,
        out_specs=(
            P("fsdp", "ctx", None),
            P("fsdp", "ctx", None),
            P("fsdp"),
            P("fsdp", None),
            P("fsdp", None),
            P("fsdp", None),
            P(None, "fsdp"),
            P("fsdp"),
            P(None, "fsdp"),
            P(None, "fsdp"),
            P("fsdp", None),
        ),
        check_vma=False,
    )
```

time: 868 us -> 300 us (0.35)
  waiting for transfers between devices: 405 us -> 103 us
  blocking collectives: 191 us -> 0 us
  matrix products: 151 us -> 0 us
  Pallas kernels: 0 us -> 67.5 us
  starting transfers between devices: 3.18 us -> 68 us
  other arithmetic: 60.6 us -> 36.6 us
  between operations: 15.7 us -> 1.15 us
  local copies, waits for them, and re-layouts: 36.2 us -> 23.8 us
    reduce_scatter x5 -> x0, waiting for transfers between devices: 310 us -> none  [the longest x1 69.5 us: on_device(): lax.psum_scatter(grad_up_w.astype(jnp.bfloat16), 'fsdp', scatter_dimensio...]
    dot_general x105 -> x0, matrix products: 151 us -> none  [the longest x12 26.6 us: per_head(): jnp.einsum('tgd,sd->gts', grad_head, value_head, preferred_element_type=j...]
    all_gather x5 -> x0, blocking collectives: 138 us -> none  [the longest x1 35.2 us: attention_weights(): lax.all_gather(query_weight, 'fsdp', axis=0, tiled=True)]
    pallas_call x0 -> x7, Pallas kernels: none -> 67.5 us  [the longest x1 20.5 us: on_device(): call(functools.partial(feed_kernel, b_labels), [low_rows, wide_rows, head...]
    ppermute x10 -> x35, starting transfers between devices: 2.25 us -> 68 us  [swap(): lax.ppermute(value, axis, [(source, source ^ bit) for source in range(cou...]
    ppermute x10 -> x35, waiting for transfers between devices: 40.9 us -> 103 us  [swap(): lax.ppermute(value, axis, [(source, source ^ bit) for source in range(cou...]
    unnamed x2 -> x0, blocking collectives: 41.1 us -> none
    unnamed x13 -> x0, waiting for transfers between devices: 31 us -> none
  transfers between devices with their start and end apart: 21 -> 35, of which waited for: 14 -> 16; matrix products, arithmetic and copies ran while one was open for 26% -> 17% of each run, Pallas kernels for 0% -> 9%
where the time goes in v1:
time: 300 us
  waiting for transfers between devices  103 us (34%)
  starting transfers between devices  68 us (23%)
  Pallas kernels  67.5 us (22%)
  other arithmetic  36.6 us (12%)
  local copies, waits for them, and re-layouts  23.8 us (8%)
    ppermute x35, waiting for transfers between devices, swap(): lax.ppermute(value, axis, [(source, source ^ bit) for source in range(cou...  103 us
    ppermute x35, starting transfers between devices, swap(): lax.ppermute(value, axis, [(source, source ^ bit) for source in range(cou...  68 us
    pallas_call x1, Pallas kernels, on_device(): call(functools.partial(feed_kernel, b_labels), [low_rows, wide_rows, head...  20.5 us
    pallas_call x1, Pallas kernels, on_device(): call(attend_back_kernel, [heads_t, slots], 10 * 4 * tokens * length * QUE...  12.3 us
    convert_element_type x13, other arithmetic, add_low(): return (left.astype(f32) + right.astype(f32)).astype(bf16)  11.5 us
    unnamed x28, local copies, waits for them, and re-layouts  11.5 us
    concatenate x9, other arithmetic, gather_slots(): stack = jnp.concatenate([stack, swap(stack, axis, bit)], axis=0)  9.8 us
    pallas_call x1, Pallas kernels, on_device(): call(attend_kernel, [shape((QUERY_WIDTH, tokens), f32), lines], 4 * 4 * t...  9.08 us
  transfers between devices with their start and end apart: 35, of which 16 were waited for; matrix products, arithmetic and copies ran while one was open for 17% of the time, Pallas kernels for 9%

profile of v1, /device:TPU:0, one launch (start us, length us, event | category | flops | bytes accessed | tf_op | source)
XLA Modules:
  0.0 300.1 jit_solution(1382684183458488107)
XLA Ops:
  5.1 4.1 %collective-permute-start.3 = (bf16[1,72,512]{2,1,0:T(8,128)(2,1)S(1)}, bf16[1,72,512]{2,1,0:T(8,128)(2,1)S(1)}, u32[]{:S(2)}, u32[]{:S(2)}) collective-permute-start(bf16[1,72,512]{2,1,0:T(8,128)(2,1)S(1)} %dynamic-slice_bitcast_fusion), channel_id=1, source_target_pairs={{0,4},{1,5},{2,6},{3,7},{4,0},{5,1},{6,2},{7,3},{8,12},{9,13},{10,... | collective-permute-start | bytes 221192 | tf_op jit(solution)/shard_map/ppermute | solution.py:39
  12.7 11.6 %collective-permute-done.11 = bf16[1,192,576]{2,1,0:T(8,128)(2,1)S(1)} collective-permute-done((bf16[1,192,576]{2,1,0:T(8,128)(2,1)S(1)}, bf16[1,192,576]{2,1,0:T(8,128)(2,1)S(1)}, u32[]{:S(2)}, u32[]{:S(2)}) %collective-permute-start.11) | collective-permute-done | bytes 221216 | tf_op jit(solution)/shard_map/ppermute | solution.py:39
  32.8 13.9 %collective-permute-done.12 = bf16[2,192,576]{2,1,0:T(8,128)(2,1)S(1)} collective-permute-done((bf16[2,192,576]{2,1,0:T(8,128)(2,1)}, bf16[2,192,576]{2,1,0:T(8,128)(2,1)S(1)}, u32[]{:S(2)}, u32[]{:S(2)}) %collective-permute-start.12) | collective-permute-done | bytes 442400 | tf_op jit(solution)/shard_map/ppermute | solution.py:39
  55.1 15.9 %collective-permute-done.13 = bf16[4,192,576]{2,1,0:T(8,128)(2,1)} collective-permute-done((bf16[4,192,576]{2,1,0:T(8,128)(2,1)}, bf16[4,192,576]{2,1,0:T(8,128)(2,1)}, u32[]{:S(2)}, u32[]{:S(2)}) %collective-permute-start.13) | collective-permute-done | bytes 884768 | tf_op jit(solution)/shard_map/ppermute | solution.py:39
  78.0 3.5 %pad_maximum_fusion.hidden = bf16[4,512,640]{2,1,0:T(8,128)(2,1)} fusion(bf16[1,512,640]{2,1,0:T(8,128)(2,1)} %bitcast.7, bf16[1,512,640]{2,1,0:T(8,128)(2,1)} %bitcast.6, bf16[1,512,640]{2,1,0:T(8,128)(2,1)} %bitcast.5, bf16[1,512,640]{2,1,0:T(8,128)(2,1)S(1)} %get-tuple-element.83), kind=kLoop, calls=%fused_computation.2 | loop fusion | flops 3932160 | bytes 5242880 | tf_op jit(solution)/shard_map/stack | solution.py:459
  83.5 8.6 %shard_map.203 = (bf16[576,512]{1,0:T(8,128)(2,1)}, bf16[384,2048]{1,0:T(8,128)(2,1)}, bf16[3,2048,128]{2,1,0:T(8,128)(2,1)}, bf16[4,512,576]{2,1,0:T(8,128)(2,1...) custom-call(s32[10]{0:T(128)} %pad_add_fusion.info, bf16[4,512,640]{2,1,0:T(8,128)(2,1)} %pad_maximum_fusion.hidden, ...), custom_call_target="tpu_custom_call" | custom-call | flops 1245708288 | tf_op jit(solution)/shard_map/pallas_call | solution.py:508
  92.1 9.1 %shard_map.204 = (f32[576,512]{1,0:T(8,128)}, f32[3,3,512]{2,1,0:T(4,128)}) custom-call(s32[10]{0:T(128)} %pad_add_fusion.info, bf16[576,512]{1,0:T(8,128)(2,1)} %get-tuple-element.35.query_t, bf16[384,2048]{1,0:T(8,128)(2,1)} %get-tuple-element.36.kv_t, bf16[3,2048,128]{2,1,0:T(8,128)(2,1)} %get-tuple-element.37.kv_rows), custom_call_target="tpu_custom_call" | custom-call | flops 9663676416 | tf_op jit(solution)/shard_map/pallas_call | solution.py:544
  101.2 4.9 %shard_map.205 = (f32[512,576]{1,0:T(8,128)}, bf16[512,576]{1,0:T(8,128)(2,1)}, bf16[576,576]{1,0:T(8,128)(2,1)}) custom-call(s32[10]{0:T(128)} %pad_add_fusion.info, bf16[512,576]{1,0:T(8,128)(2,1)} %bitcast.68, f32[576,512]{1,0:T(8,128)} %get-tuple-element.38.attended_t, bf16[8,144,576]{2,1,0:T(8,128)(2,1)} %copy-done.2, ...), custom_call_target="tpu_custom_call" | custom-call | flops 339738624 | tf_op jit(solution)/shard_map/pallas_call | solution.py:561
  106.2 20.5 %shard_map.206 = (bf16[512,576]{1,0:T(8,128)(2,1)}, f32[512,576]{1,0:T(8,128)}, bf16[576,512]{1,0:T(8,128)(2,1)}, f32[3,3,512]{2,1,0:T(4,128)}, bf16[8,192,576]{...) custom-call(s32[10]{0:T(128)} %pad_add_fusion.info, ...), custom_call_target="tpu_custom_call" | custom-call | flops 8153726976 | tf_op jit(solution)/shard_map/pallas_call | solution.py:572
  126.7 12.3 %shard_map.207 = (bf16[576,512]{1,0:T(8,128)(2,1)}, bf16[4,3,128,512]{3,2,1,0:T(8,128)(2,1)}) custom-call(s32[10]{0:T(128)} %pad_add_fusion.info, bf16[576,512]{1,0:T(8,128)(2,1)} %get-tuple-element.35.query_t, bf16[384,2048]{1,0:T(8,128)(2,1)} %get-tuple-element.36.kv_t, bf16[3,2048,128]{2,1,0:T(8,128)(2,1)} %get-tuple-element.37.kv_rows, ...), custom_call_target="tpu_custom_call" | custom-call | flops 24159191040 | tf_op jit(solution)/shard_map/pallas_call | solution.py:616
  139.0 7.2 %shard_map.209 = (bf16[8,72,512]{2,1,0:T(8,128)(2,1)}, bf16[8,72,512]{2,1,0:T(8,128)(2,1)}) custom-call(s32[10]{0:T(128)} %pad_add_fusion.info, bf16[576,512]{1,0:T(8,128)(2,1)} %get-tuple-element.47.grad_query_t, bf16[4,3,128,512]{3,2,1,0:T(8,128)(2,1)} %get-tuple-element.48.grad_kv_t, bf16[4,512,576]{2,1,0:T(8,128)(2,1)} %get-tuple-element.51.normed, ...), custom_call_target="tpu_custom_call" | custom-call | flops 1245708288 | tf_op jit(solution)/shard_map/pallas_call | solution.py:640
  146.2 27.7 %collective-permute-start.17 = (bf16[8,72,512]{2,1,0:T(8,128)(2,1)}, bf16[8,72,512]{2,1,0:T(8,128)(2,1)S(1)}, u32[]{:S(2)}, u32[]{:S(2)}) collective-permute-start(bf16[8,72,512]{2,1,0:T(8,128)(2,1)} %get-tuple-element.54), channel_id=1, source_target_pairs={{0,8},{8,0},{16,24},{24,16},{1,9},{9,1},{17,25},{25,17},{2,10},{10... | collective-permute-start | bytes 1769480 | tf_op jit(solution)/shard_map/ppermute | solution.py:39
  177.6 8.7 %collective-permute-done.18 = bf16[4,72,512]{2,1,0:T(8,128)(2,1)S(1)} collective-permute-done((bf16[4,72,512]{2,1,0:T(8,128)(2,1)S(1)}, bf16[4,72,512]{2,1,0:T(8,128)(2,1)S(1)}, u32[]{:S(2)}, u32[]{:S(2)}) %collective-permute-start.18) | collective-permute-done | bytes 294944 | tf_op jit(solution)/shard_map/ppermute | solution.py:39
  189.7 3.0 collective-permute-done.19
  193.6 12.2 %collective-permute-start.20 = (bf16[1,72,512]{2,1,0:T(8,128)(2,1)S(1)}, bf16[1,72,512]{2,1,0:T(8,128)(2,1)S(1)}, u32[]{:S(2)}, u32[]{:S(2)}) collective-permute-start(bf16[1,72,512]{2,1,0:T(8,128)(2,1)S(1)} %slice.185), channel_id=1, source_target_pairs={{0,4},{1,5},{2,6},{3,7},{4,0},{5,1},{6,2},{7,3},{8,12},{9,13},{10,... | collective-permute-start | bytes 221192 | tf_op jit(solution)/shard_map/ppermute | solution.py:39
  210.4 3.1 %collective-permute-done.21 = bf16[72,512]{1,0:T(8,128)(2,1)S(1)} collective-permute-done((bf16[72,512]{1,0:T(8,128)(2,1)S(1)}, bf16[72,512]{1,0:T(8,128)(2,1)S(1)}, u32[]{:S(2)}, u32[]{:S(2)}) %collective-permute-start.21) | collective-permute-done | bytes 73760 | tf_op jit(solution)/shard_map/ppermute | solution.py:39
  219.8 4.8 %shard_map.208 = f32[512,576]{1,0:T(8,128)} custom-call(bf16[576,512]{1,0:T(8,128)(2,1)} %get-tuple-element.47.grad_query_t, bf16[384,512]{1,0:T(8,128)(2,1)} %bitcast.77, bf16[1024,576]{1,0:T(8,128)(2,1)} %get-tuple-element.49.weight_t, bf16[512,576]{1,0:T(8,128)(2,1)} %bitcast.69, f32[512,576]{1,0:T(8,128)} %get-tuple-element.50.grad_middle, ...), custom_call_target="tpu_custom_call" | custom-call | flops 566231040 | tf_op jit(solution)/shard_map/pallas_call | solution.py:662
  231.9 3.8 %collective-permute-done.24 = bf16[4,144,576]{2,1,0:T(8,128)(2,1)} collective-permute-done((bf16[4,144,576]{2,1,0:T(8,128)(2,1)}, bf16[4,144,576]{2,1,0:T(8,128)(2,1)}, u32[]{:S(2)}, u32[]{:S(2)}) %collective-permute-start.24) | collective-permute-done | bytes 663584 | tf_op jit(solution)/shard_map/ppermute | solution.py:39
  238.6 3.4 %collective-permute-start.25 = (bf16[2,144,576]{2,1,0:T(8,128)(2,1)}, bf16[2,144,576]{2,1,0:T(8,128)(2,1)}, u32[]{:S(2)}, u32[]{:S(2)}) collective-permute-start(bf16[2,144,576]{2,1,0:T(8,128)(2,1)} %slice.193), channel_id=1, source_target_pairs={{0,4},{1,5},{2,6},{3,7},{4,0},{5,1},{6,2},{7,3},{8,12},{9,13},{10,... | collective-permute-start | bytes 995336 | tf_op jit(solution)/shard_map/ppermute | solution.py:39
  244.6 14.3 %collective-permute-done.25 = bf16[2,144,576]{2,1,0:T(8,128)(2,1)} collective-permute-done((bf16[2,144,576]{2,1,0:T(8,128)(2,1)}, bf16[2,144,576]{2,1,0:T(8,128)(2,1)}, u32[]{:S(2)}, u32[]{:S(2)}) %collective-permute-start.25) | collective-permute-done | bytes 331808 | tf_op jit(solution)/shard_map/ppermute | solution.py:39
  269.4 5.6 %collective-permute-done.31 = bf16[2,192,576]{2,1,0:T(8,128)(2,1)S(1)} collective-permute-done((bf16[2,192,576]{2,1,0:T(8,128)(2,1)S(1)}, bf16[2,192,576]{2,1,0:T(8,128)(2,1)S(1)}, u32[]{:S(2)}, u32[]{:S(2)}) %collective-permute-start.31) | collective-permute-done | bytes 442400 | tf_op jit(solution)/shard_map/ppermute | solution.py:39
  275.1 3.1 %collective-permute-start.32 = (bf16[1,192,576]{2,1,0:T(8,128)(2,1)S(1)}, bf16[1,192,576]{2,1,0:T(8,128)(2,1)S(1)}, u32[]{:S(2)}, u32[]{:S(2)}) collective-permute-start(bf16[1,192,576]{2,1,0:T(8,128)(2,1)S(1)} %slice.204), channel_id=1, source_target_pairs={{0,4},{1,5},{2,6},{3,7},{4,0},{5,1},{6,2},{7,3},{8,12},{9,13},{10,... | collective-permute-start | bytes 663560 | tf_op jit(solution)/shard_map/ppermute | solution.py:39
  278.3 10.4 %collective-permute-done.32 = bf16[1,192,576]{2,1,0:T(8,128)(2,1)S(1)} collective-permute-done((bf16[1,192,576]{2,1,0:T(8,128)(2,1)S(1)}, bf16[1,192,576]{2,1,0:T(8,128)(2,1)S(1)}, u32[]{:S(2)}, u32[]{:S(2)}) %collective-permute-start.32) | collective-permute-done | bytes 221216 | tf_op jit(solution)/shard_map/ppermute | solution.py:39
  289.7 6.1 %collective-permute-done.33 = bf16[192,576]{1,0:T(8,128)(2,1)S(1)} collective-permute-done((bf16[192,576]{1,0:T(8,128)(2,1)S(1)}, bf16[192,576]{1,0:T(8,128)(2,1)S(1)}, u32[]{:S(2)}, u32[]{:S(2)}) %collective-permute-start.33) | collective-permute-done | bytes 221216 | tf_op jit(solution)/shard_map/ppermute | solution.py:39
  (159 shorter events, 80.9 us)
Async XLA Ops:
  5.1 24.1 %collective-permute-start.3 = (bf16[1,72,512]{2,1,0:T(8,128)(2,1)S(1)}, bf16[1,72,512]{2,1,0:T(8,128)(2,1)S(1)}, u32[]{:S(2)}, u32[]{:S(2)}) collective-permute-start(bf16[1,72,512]{2,1,0:T(8,128)(2,1)S(1)} %dynamic-slice_bitcast_fusion), channel_id=1, source_target_pairs={{0,4},{1,5},{2,6},{3,7},{4,0},{5,1},{6,2},{7,3},{8,12},{9,13},{10,... | collective-permute-start | bytes 221192 | tf_op jit(solution)/shard_map/ppermute | solution.py:39
  10.6 13.6 %collective-permute-start.11 = (bf16[1,192,576]{2,1,0:T(8,128)(2,1)S(1)}, bf16[1,192,576]{2,1,0:T(8,128)(2,1)S(1)}, u32[]{:S(2)}, u32[]{:S(2)}) collective-permute-start(bf16[1,192,576]{2,1,0:T(8,128)(2,1)S(1)} %bitcast.73), channel_id=1, source_target_pairs={{0,4},{1,5},{2,6},{3,7},{4,0},{5,1},{6,2},{7,3},{8,12},{9,13},{10,... | collective-permute-start | bytes 663560 | tf_op jit(solution)/shard_map/ppermute | solution.py:39
  10.8 20.4 %collective-permute-start.7 = (bf16[1,144,576]{2,1,0:T(8,128)(2,1)S(1)}, bf16[1,144,576]{2,1,0:T(8,128)(2,1)S(1)}, u32[]{:S(2)}, u32[]{:S(2)}) collective-permute-start(bf16[1,144,576]{2,1,0:T(8,128)(2,1)S(1)} %maximum_bitcast_fusion.2), channel_id=1, source_target_pairs={{0,1},{1,0},{2,3},{3,2},{4,5},{5,4},{6,7},{7,6},{8,9},{9,8},{10,11... | collective-permute-start | bytes 497672 | tf_op jit(solution)/shard_map/ppermute | solution.py:39
  25.1 21.7 %collective-permute-start.12 = (bf16[2,192,576]{2,1,0:T(8,128)(2,1)}, bf16[2,192,576]{2,1,0:T(8,128)(2,1)S(1)}, u32[]{:S(2)}, u32[]{:S(2)}) collective-permute-start(bf16[2,192,576]{2,1,0:T(8,128)(2,1)} %pad_maximum_fusion.8), channel_id=1, source_target_pairs={{0,2},{1,3},{2,0},{3,1},{4,6},{5,7},{6,4},{7,5},{8,10},{9,11},{10,... | collective-permute-start | bytes 1327112 | tf_op jit(solution)/shard_map/ppermute | solution.py:39
  27.7 50.3 %collective-permute-start = (bf16[512,640]{1,0:T(8,128)(2,1)}, bf16[512,640]{1,0:T(8,128)(2,1)}, u32[]{:S(2)}, u32[]{:S(2)}) collective-permute-start(bf16[512,640]{1,0:T(8,128)(2,1)} %get-tuple-element.84), channel_id=1, source_target_pairs={{0,8},{8,0},{16,24},{24,16},{1,9},{9,1},{17,25},{25,17},{2,10},{10... | collective-permute-start | bytes 1966088 | tf_op jit(solution)/shard_map/ppermute | solution.py:39
  27.7 24.4 %collective-permute-start.1 = (bf16[512,640]{1,0:T(8,128)(2,1)}, bf16[512,640]{1,0:T(8,128)(2,1)}, u32[]{:S(2)}, u32[]{:S(2)}) collective-permute-start(bf16[512,640]{1,0:T(8,128)(2,1)} %get-tuple-element.84), channel_id=1, source_target_pairs={{0,16},{8,24},{16,0},{24,8},{1,17},{9,25},{17,1},{25,9},{2,18},{10... | collective-permute-start | bytes 1966088 | tf_op jit(solution)/shard_map/ppermute | solution.py:39
  29.2 20.2 %collective-permute-start.4 = (bf16[2,72,512]{2,1,0:T(8,128)(2,1)S(1)}, bf16[2,72,512]{2,1,0:T(8,128)(2,1)S(1)}, u32[]{:S(2)}, u32[]{:S(2)}) collective-permute-start(bf16[2,72,512]{2,1,0:T(8,128)(2,1)S(1)} %pad_maximum_fusion.14), channel_id=1, source_target_pairs={{0,2},{1,3},{2,0},{3,1},{4,6},{5,7},{6,4},{7,5},{8,10},{9,11},{10,... | collective-permute-start | bytes 442376 | tf_op jit(solution)/shard_map/ppermute | solution.py:39
  31.3 19.4 %collective-permute-start.8 = (bf16[2,144,576]{2,1,0:T(8,128)(2,1)S(1)}, bf16[2,144,576]{2,1,0:T(8,128)(2,1)S(1)}, u32[]{:S(2)}, u32[]{:S(2)}) collective-permute-start(bf16[2,144,576]{2,1,0:T(8,128)(2,1)S(1)} %pad_maximum_fusion.10), channel_id=1, source_target_pairs={{0,4},{1,5},{2,6},{3,7},{4,0},{5,1},{6,2},{7,3},{8,12},{9,13},{10,... | collective-permute-start | bytes 995336 | tf_op jit(solution)/shard_map/ppermute | solution.py:39
  47.9 23.1 %collective-permute-start.13 = (bf16[4,192,576]{2,1,0:T(8,128)(2,1)}, bf16[4,192,576]{2,1,0:T(8,128)(2,1)}, u32[]{:S(2)}, u32[]{:S(2)}) collective-permute-start(bf16[4,192,576]{2,1,0:T(8,128)(2,1)} %pad_maximum_fusion.3), channel_id=1, source_target_pairs={{0,1},{1,0},{2,3},{3,2},{4,5},{5,4},{6,7},{7,6},{8,9},{9,8},{10,11... | collective-permute-start | bytes 2654216 | tf_op jit(solution)/shard_map/ppermute | solution.py:39
  50.2 24.0 %collective-permute-start.5 = (bf16[4,72,512]{2,1,0:T(8,128)(2,1)}, bf16[4,72,512]{2,1,0:T(8,128)(2,1)}, u32[]{:S(2)}, u32[]{:S(2)}) collective-permute-start(bf16[4,72,512]{2,1,0:T(8,128)(2,1)} %pad_maximum_fusion.11), channel_id=1, source_target_pairs={{0,1},{1,0},{2,3},{3,2},{4,5},{5,4},{6,7},{7,6},{8,9},{9,8},{10,11... | collective-permute-start | bytes 884744 | tf_op jit(solution)/shard_map/ppermute | solution.py:39
  51.7 24.6 %collective-permute-start.9 = (bf16[4,144,576]{2,1,0:T(8,128)(2,1)}, bf16[4,144,576]{2,1,0:T(8,128)(2,1)}, u32[]{:S(2)}, u32[]{:S(2)}) collective-permute-start(bf16[4,144,576]{2,1,0:T(8,128)(2,1)} %pad_maximum_fusion.5), channel_id=1, source_target_pairs={{0,2},{1,3},{2,0},{3,1},{4,6},{5,7},{6,4},{7,5},{8,10},{9,11},{10,... | collective-permute-start | bytes 1990664 | tf_op jit(solution)/shard_map/ppermute | solution.py:39
  52.1 25.9 %collective-permute-start.2 = (bf16[512,640]{1,0:T(8,128)(2,1)}, bf16[512,640]{1,0:T(8,128)(2,1)}, u32[]{:S(2)}, u32[]{:S(2)}) collective-permute-start(bf16[512,640]{1,0:T(8,128)(2,1)} %collective-permute-done.1), channel_id=1, source_target_pairs={{0,8},{8,0},{16,24},{24,16},{1,9},{9,1},{17,25},{25,17},{2,10},{10... | collective-permute-start | bytes 1966088 | tf_op jit(solution)/shard_map/ppermute | solution.py:39
  73.9 32.3 %collective-permute-start.14 = (bf16[8,192,576]{2,1,0:T(8,128)(2,1)}, bf16[8,192,576]{2,1,0:T(8,128)(2,1)}, u32[]{:S(2)}, u32[]{:S(2)}) collective-permute-start(bf16[8,192,576]{2,1,0:T(8,128)(2,1)} %pad_maximum_fusion.1.a_own), channel_id=1, source_target_pairs={{0,8},{8,0},{16,24},{24,16},{1,9},{9,1},{17,25},{25,17},{2,10},{10... | collective-permute-start | bytes 5308424 | tf_op jit(solution)/shard_map/ppermute | solution.py:39
  77.6 23.6 %collective-permute-start.10 = (bf16[8,144,576]{2,1,0:T(8,128)(2,1)S(1)}, bf16[8,144,576]{2,1,0:T(8,128)(2,1)}, u32[]{:S(2)}, u32[]{:S(2)}) collective-permute-start(bf16[8,144,576]{2,1,0:T(8,128)(2,1)S(1)} %pad_maximum_fusion.2.b_own), channel_id=1, source_target_pairs={{0,8},{8,0},{16,24},{24,16},{1,9},{9,1},{17,25},{25,17},{2,10},{10... | collective-permute-start | bytes 3981320 | tf_op jit(solution)/shard_map/ppermute | solution.py:39
  146.2 29.5 %collective-permute-start.17 = (bf16[8,72,512]{2,1,0:T(8,128)(2,1)}, bf16[8,72,512]{2,1,0:T(8,128)(2,1)S(1)}, u32[]{:S(2)}, u32[]{:S(2)}) collective-permute-start(bf16[8,72,512]{2,1,0:T(8,128)(2,1)} %get-tuple-element.54), channel_id=1, source_target_pairs={{0,8},{8,0},{16,24},{24,16},{1,9},{9,1},{17,25},{25,17},{2,10},{10... | collective-permute-start | bytes 1769480 | tf_op jit(solution)/shard_map/ppermute | solution.py:39
  177.1 28.8 %collective-permute-start.15 = (bf16[2,3,128,512]{3,2,1,0:T(8,128)(2,1)S(1)}, bf16[2,3,128,512]{3,2,1,0:T(8,128)(2,1)S(1)}, u32[]{:S(2)}, u32[]{:S(2)}) collective-permute-start(bf16[2,3,128,512]{3,2,1,0:T(8,128)(2,1)S(1)} %slice_bitcast_fusion), channel_id=1, source_target_pairs={{0,8},{8,0},{16,24},{24,16},{1,9},{9,1},{17,25},{25,17},{2,10},{10... | collective-permute-start | bytes 2359304 | tf_op jit(solution)/shard_map/ppermute | solution.py:39
  187.0 26.6 %collective-permute-start.23 = (bf16[8,144,576]{2,1,0:T(8,128)(2,1)}, bf16[8,144,576]{2,1,0:T(8,128)(2,1)}, u32[]{:S(2)}, u32[]{:S(2)}) collective-permute-start(bf16[8,144,576]{2,1,0:T(8,128)(2,1)} %get-tuple-element.56), channel_id=1, source_target_pairs={{0,8},{8,0},{16,24},{24,16},{1,9},{9,1},{17,25},{25,17},{2,10},{10... | collective-permute-start | bytes 3981320 | tf_op jit(solution)/shard_map/ppermute | solution.py:39
  189.2 38.2 %collective-permute-start.29 = (bf16[8,192,576]{2,1,0:T(8,128)(2,1)}, bf16[8,192,576]{2,1,0:T(8,128)(2,1)}, u32[]{:S(2)}, u32[]{:S(2)}) collective-permute-start(bf16[8,192,576]{2,1,0:T(8,128)(2,1)} %get-tuple-element.58), channel_id=1, source_target_pairs={{0,8},{8,0},{16,24},{24,16},{1,9},{9,1},{17,25},{25,17},{2,10},{10... | collective-permute-start | bytes 5308424 | tf_op jit(solution)/shard_map/ppermute | solution.py:39
  193.6 14.6 %collective-permute-start.20 = (bf16[1,72,512]{2,1,0:T(8,128)(2,1)S(1)}, bf16[1,72,512]{2,1,0:T(8,128)(2,1)S(1)}, u32[]{:S(2)}, u32[]{:S(2)}) collective-permute-start(bf16[1,72,512]{2,1,0:T(8,128)(2,1)S(1)} %slice.185), channel_id=1, source_target_pairs={{0,4},{1,5},{2,6},{3,7},{4,0},{5,1},{6,2},{7,3},{8,12},{9,13},{10,... | collective-permute-start | bytes 221192 | tf_op jit(solution)/shard_map/ppermute | solution.py:39
  213.5 28.5 %collective-permute-start.22 = (bf16[72,512]{1,0:T(8,128)(2,1)S(1)}, bf16[72,512]{1,0:T(8,128)(2,1)}, u32[]{:S(2)}, u32[]{:S(2)}) collective-permute-start(bf16[72,512]{1,0:T(8,128)(2,1)S(1)} %add_convert_fusion.13), channel_id=1, source_target_pairs={{0,8},{8,0},{16,24},{24,16},{1,9},{9,1},{17,25},{25,17},{2,10},{10... | collective-permute-start | bytes 221192 | tf_op jit(solution)/shard_map/ppermute | solution.py:39
  216.4 19.2 %collective-permute-start.24 = (bf16[4,144,576]{2,1,0:T(8,128)(2,1)}, bf16[4,144,576]{2,1,0:T(8,128)(2,1)}, u32[]{:S(2)}, u32[]{:S(2)}) collective-permute-start(bf16[4,144,576]{2,1,0:T(8,128)(2,1)} %slice.191), channel_id=1, source_target_pairs={{0,2},{1,3},{2,0},{3,1},{4,6},{5,7},{6,4},{7,5},{8,10},{9,11},{10,... | collective-permute-start | bytes 1990664 | tf_op jit(solution)/shard_map/ppermute | solution.py:39
  231.1 30.1 %collective-permute-start.30 = (bf16[4,192,576]{2,1,0:T(8,128)(2,1)}, bf16[4,192,576]{2,1,0:T(8,128)(2,1)}, u32[]{:S(2)}, u32[]{:S(2)}) collective-permute-start(bf16[4,192,576]{2,1,0:T(8,128)(2,1)} %slice.200), channel_id=1, source_target_pairs={{0,1},{1,0},{2,3},{3,2},{4,5},{5,4},{6,7},{7,6},{8,9},{9,8},{10,11... | collective-permute-start | bytes 2654216 | tf_op jit(solution)/shard_map/ppermute | solution.py:39
  238.6 20.2 %collective-permute-start.25 = (bf16[2,144,576]{2,1,0:T(8,128)(2,1)}, bf16[2,144,576]{2,1,0:T(8,128)(2,1)}, u32[]{:S(2)}, u32[]{:S(2)}) collective-permute-start(bf16[2,144,576]{2,1,0:T(8,128)(2,1)} %slice.193), channel_id=1, source_target_pairs={{0,4},{1,5},{2,6},{3,7},{4,0},{5,1},{6,2},{7,3},{8,12},{9,13},{10,... | collective-permute-start | bytes 995336 | tf_op jit(solution)/shard_map/ppermute | solution.py:39
  275.1 13.6 %collective-permute-start.32 = (bf16[1,192,576]{2,1,0:T(8,128)(2,1)S(1)}, bf16[1,192,576]{2,1,0:T(8,128)(2,1)S(1)}, u32[]{:S(2)}, u32[]{:S(2)}) collective-permute-start(bf16[1,192,576]{2,1,0:T(8,128)(2,1)S(1)} %slice.204), channel_id=1, source_target_pairs={{0,4},{1,5},{2,6},{3,7},{4,0},{5,1},{6,2},{7,3},{8,12},{9,13},{10,... | collective-permute-start | bytes 663560 | tf_op jit(solution)/shard_map/ppermute | solution.py:39
  (21 other events, 200.9 us)

commit v2 on v1

v2 whole, which is shorter than its diff:
```python
import functools
import math

import jax
import jax.numpy as jnp
from jax import lax
from jax.experimental import pallas as pl
from jax.experimental.pallas import tpu as pltpu
from jax.sharding import PartitionSpec as P

QUERY_HEADS = 9
KEY_VALUE_HEADS = 3
HEAD_FEATURES = 64
GROUP = QUERY_HEADS // KEY_VALUE_HEADS
HALF = HEAD_FEATURES // 2
PAIR = 2 * HEAD_FEATURES
RUN = 256
OWN = 2
QUERY_WIDTH = QUERY_HEADS * HEAD_FEATURES
KV_WIDTH = KEY_VALUE_HEADS * PAIR
PROJECTED = QUERY_WIDTH + KV_WIDTH
PADDED = 1024
PART = PADDED // 2
MARK = 16
SCALE = 1.0 / math.sqrt(HEAD_FEATURES)

rms_epsilon = 1e-05
rope_base = 100000.0
score_after_mask = -1e30
bf16 = jnp.bfloat16
f32 = jnp.float32
VMEM_BYTES = 60 * 1024 * 1024


def dot(left, right, left_dim, right_dim):
    return lax.dot_general(
        left, right, (((left_dim,), (right_dim,)), ((), ())), preferred_element_type=f32
    )


def swap(value, axis, bit):
    count = lax.axis_size(axis)
    return lax.ppermute(value, axis, [(source, source ^ bit) for source in range(count)])


def axis_bits(axis):
    count = lax.axis_size(axis)
    return [1 << place for place in range(count.bit_length() - 1)]


def tie(*values):
    return lax.optimization_barrier(values)


def gather_all(value, bits):
    found = {0: value}
    for bit in bits:
        for label in list(found):
            found[label ^ bit] = swap(found[label], "ctx", bit)
    return [found[label] for label in range(len(found))]


def add_low(left, right):
    return (left.astype(f32) + right.astype(f32)).astype(bf16)


def rotate(rows, cosine, sine):
    first, second = rows[:HALF], rows[HALF:]
    return jnp.concatenate([first * cosine - second * sine, second * cosine + first * sine], axis=0)


def rotate_back(rows, cosine, sine):
    first, second = rows[:HALF], rows[HALF:]
    return jnp.concatenate([first * cosine + second * sine, second * cosine - first * sine], axis=0)


def run_slice(run):
    return pl.ds(pl.multiple_of(run * RUN, RUN), RUN)


def part_slice(j):
    return slice(j * RUN, (j + 1) * RUN)


def head_slice(h):
    return slice(h * HEAD_FEATURES, (h + 1) * HEAD_FEATURES)


def own_runs(ctx, runs):
    return (ctx, runs - 1 - ctx)


def column_of(row):
    size = row.shape[1]
    same = lax.broadcasted_iota(jnp.int32, (size, size), 0) == lax.broadcasted_iota(
        jnp.int32, (size, size), 1
    )
    return jnp.sum(jnp.where(same, jnp.broadcast_to(row, (size, size)), 0.0), axis=1, keepdims=True)


def row_of(column):
    size = column.shape[0]
    same = lax.broadcasted_iota(jnp.int32, (size, size), 0) == lax.broadcasted_iota(
        jnp.int32, (size, size), 1
    )
    return jnp.sum(jnp.where(same, jnp.broadcast_to(column, (size, size)), 0.0), axis=0, keepdims=True)


def norm_scale(rows):
    return lax.rsqrt(jnp.mean(rows * rows, axis=0, keepdims=True) + rms_epsilon)


def prepare_kernel(
    info, hidden, positions, query_w, key_w, value_w, attn_gain, mlp_gain, gate_w, up_w, down_w, out_w,
    extended, w_mine, a_mine, b_mine, columns, out_rows,
):
    core = info[1]
    width, tokens = hidden.shape
    extended[:width, :] = hidden[...]
    marks = (positions[...] // RUN).astype(f32)
    extended[width:, :] = jnp.broadcast_to(marks, (MARK, tokens)).astype(bf16)

    columns[:, PROJECTED - HEAD_FEATURES :] = jnp.zeros(
        (columns.shape[0], PADDED - PROJECTED + HEAD_FEATURES), f32
    )
    columns[:, :QUERY_WIDTH] = query_w[...].astype(f32)
    for g in range(KEY_VALUE_HEADS):
        start = QUERY_WIDTH + g * PAIR
        columns[:, start : start + HEAD_FEATURES] = key_w[:, head_slice(g)].astype(f32)
        columns[:, start + HEAD_FEATURES : start + PAIR] = value_w[:, head_slice(g)].astype(f32)
    columns[:, PROJECTED : PROJECTED + 1] = column_of(attn_gain[...].astype(f32))
    columns[:, PROJECTED + 1 : PROJECTED + 2] = column_of(mlp_gain[...].astype(f32))
    w_mine[...] = columns[:, pl.ds(pl.multiple_of(core * PART, PART), PART)].astype(bf16)

    ff_rows = down_w.shape[0]
    unit_a, unit_b = ff_rows // 3, ff_rows // 6
    half = out_rows.shape[0] // 2
    for place, source in enumerate((gate_w, up_w, down_w)):
        rows = pl.ds(pl.multiple_of(core * unit_a, 16), unit_a)
        a_mine[place * unit_a : (place + 1) * unit_a, :] = source[rows, :]
        rows = pl.ds(pl.multiple_of(2 * unit_a + core * unit_b, 16), unit_b)
        b_mine[place * unit_b : (place + 1) * unit_b, :] = source[rows, :]
    out_rows[...] = jnp.zeros_like(out_rows)
    out_rows[: out_w.shape[0], :] = out_w[...].astype(f32)
    b_mine[3 * unit_b :, :] = out_rows[pl.ds(pl.multiple_of(core * half, 16), half), :].astype(bf16)


def project_kernel(blocks, labels, info, *refs):
    exts, refs = refs[:blocks], refs[blocks:]
    stacks, refs = refs[: 2 * len(labels)], refs[2 * len(labels) :]
    (
        cosine, sine,
        query_t, kv_t, kv_rows, normed_t, weight, hidden_own, order,
        sorted_runs, weight_t, pieces,
    ) = refs
    step = pl.program_id(0)
    width = hidden_own.shape[0]
    runs = blocks * OWN
    shards = pieces.shape[1]

    def normalized(run):
        rows = sorted_runs[run].astype(f32)
        gain = weight[:, PROJECTED : PROJECTED + 1].astype(f32)
        return (rows * norm_scale(rows) * gain).astype(bf16)

    @pl.when(step == 0)
    def _():
        me, core, ctx = info[0], info[1], info[2]
        for r in range(blocks):
            for j in range(OWN):
                mark = exts[r][width : width + MARK, part_slice(j)].astype(f32)
                run = jnp.max(mark).astype(jnp.int32)
                order[r * OWN + j] = run
                sorted_runs[run] = exts[r][:width, part_slice(j)]
        for i, group in enumerate(labels):
            for slot, label in enumerate(group):
                pieces[core, me ^ label] = stacks[i][slot]
                pieces[1 - core, me ^ label] = stacks[len(labels) + i][slot]
        for side in range(2):
            whole = jnp.concatenate([pieces[side, s].astype(f32) for s in range(shards)], axis=0)
            weight[:, side * PART : (side + 1) * PART] = whole.astype(bf16)
            weight_t[side * PART : (side + 1) * PART, :] = whole.T.astype(bf16)
        for j, run in enumerate(own_runs(ctx, runs)):
            hidden_own[:, part_slice(j)] = sorted_runs[run]
            queries = dot(weight_t[:QUERY_WIDTH, :], normalized(run), 1, 0)
            cos, sin = cosine[:, run_slice(run)], sine[:, run_slice(run)]
            for h in range(QUERY_HEADS):
                query_t[head_slice(h), part_slice(j)] = (
                    rotate(queries[head_slice(h)], cos, sin) * SCALE
                ).astype(bf16)

    for j in range(OWN):
        run = step * OWN + j
        normed = normalized(run)
        normed_t[:, part_slice(j)] = normed
        kv = dot(weight_t[QUERY_WIDTH:PROJECTED, :], normed, 1, 0)
        cos, sin = cosine[:, run_slice(run)], sine[:, run_slice(run)]
        for g in range(KEY_VALUE_HEADS):
            block = kv[g * PAIR : (g + 1) * PAIR]
            block = jnp.concatenate(
                [rotate(block[:HEAD_FEATURES], cos, sin), block[HEAD_FEATURES:]], axis=0
            )
            kv_t[g * PAIR : (g + 1) * PAIR, part_slice(j)] = block.astype(bf16)
            kv_rows[g, part_slice(j), :] = block.T.astype(bf16)


def side_by_side(ref, j):
    return jnp.concatenate([ref[head_slice(h), part_slice(j)] for h in range(GROUP)], axis=1)


def causal():
    size = (RUN, GROUP * RUN)
    keys = lax.broadcasted_iota(jnp.int32, size, 0)
    queries = lax.broadcasted_iota(jnp.int32, size, 1) & (RUN - 1)
    return keys <= queries


def attend_kernel(info, query_t, kv_t, kv_rows, attended_t, log_totals, maxima, totals, sums):
    runs = kv_rows.shape[1] // RUN
    for j, own in enumerate(own_runs(info[2], runs)):
        query = side_by_side(query_t, j)
        query = jnp.concatenate([query, jnp.zeros_like(query)], axis=0)
        here = run_slice(own)
        scores = jnp.where(causal(), dot(kv_rows[0, here, :], query, 1, 0), score_after_mask)
        top = jnp.max(scores, axis=0, keepdims=True)
        weights = jnp.exp(scores - top)
        maxima[...] = top
        totals[...] = jnp.sum(weights, axis=0, keepdims=True)
        sums[...] = dot(kv_t[HEAD_FEATURES:, here], weights.astype(bf16), 1, 0)

        def advance(place, nothing):
            scores = dot(kv_rows[0, run_slice(place), :], query, 1, 0)
            before = maxima[...]
            top = jnp.maximum(before, jnp.max(scores, axis=0, keepdims=True))
            factor = jnp.exp(before - top)
            weights = jnp.exp(scores - top)
            maxima[...] = top
            totals[...] = totals[...] * factor + jnp.sum(weights, axis=0, keepdims=True)
            sums[...] = sums[...] * factor + dot(
                kv_t[HEAD_FEATURES:, run_slice(place)], weights.astype(bf16), 1, 0
            )
            return nothing

        lax.fori_loop(0, own, advance, 0)
        result = sums[...] / totals[...]
        logs = maxima[...] + jnp.log(totals[...])
        for h in range(GROUP):
            attended_t[head_slice(h), part_slice(j)] = result[:, part_slice(h)]
            log_totals[0, h : h + 1, part_slice(j)] = logs[:, part_slice(h)]


def middle_kernel(
    labels, info, hidden, attended_t, weight, b0, b1, b2, b3, middle_out, normed_out, out_weight, pieces
):
    me, core = info[0], info[1]
    half = pieces.shape[2]
    first = b0.shape[1] - half
    width = hidden.shape[0]
    shards = pieces.shape[1]
    shard_rows = width // shards
    for group, own, pair in zip(labels, (b0, b1), (b2, b3)):
        for slot, label in enumerate(group):
            pieces[core, me ^ label] = own[slot, first:, :]
            pieces[1 - core, me ^ label] = pair[slot, first:, :]
    parts = []
    for s in range(shards):
        parts.append(pieces[0, s].astype(f32)[: min(half, shard_rows)])
        if shard_rows > half:
            parts.append(pieces[1, s].astype(f32)[: shard_rows - half])
    full = jnp.concatenate(parts, axis=0).astype(bf16)
    out_weight[...] = full
    middle = hidden[...].astype(f32) + dot(full, attended_t[...].astype(bf16), 1, 0)
    middle_out[...] = middle
    gain = weight[:, PROJECTED + 1 : PROJECTED + 2].astype(f32)
    normed_out[...] = (middle * norm_scale(middle) * gain).astype(bf16)


def feed_chunk(sources, targets, unit, normed, out_grad, total, back):
    width = normed.shape[0]
    slots = sources[0].shape[0]

    def joined(place):
        rows = slice(place * unit, (place + 1) * unit)
        return jnp.concatenate([s[:, rows, :].reshape(slots * unit, width) for s in sources], axis=0)

    gate_w, up_w, down_w = joined(0), joined(1), joined(2)
    gate = dot(gate_w, normed[...], 1, 0)
    up = dot(up_w, normed[...], 1, 0)
    sigmoid = jax.nn.sigmoid(gate)
    silu = gate * sigmoid
    activated = (silu * up).astype(bf16)
    grad_act = dot(down_w, out_grad[...], 1, 0)
    grad_gate = (grad_act * up * sigmoid * (1.0 + gate * (1.0 - sigmoid))).astype(bf16)
    grad_up = (grad_act * silu).astype(bf16)
    total[...] += dot(down_w, activated, 0, 0)
    back[...] += dot(gate_w, grad_gate, 0, 0) + dot(up_w, grad_up, 0, 0)
    for place, (left, right) in enumerate(
        ((grad_gate, normed), (grad_up, normed), (activated, out_grad))
    ):
        result = dot(left, right[...], 1, 1).astype(bf16)
        for i, target in enumerate(targets):
            lines = result[i * slots * unit : (i + 1) * slots * unit]
            target[:, place * unit : (place + 1) * unit, :] = lines.reshape(slots, unit, width)


def feed_first_kernel(blocks, info, order, *refs):
    grads, refs = refs[:blocks], refs[blocks:]
    (
        normed, middle, b0, b1, b2, b3,
        out_grad, total, back, g0, g1, g2, g3,
    ) = refs
    ctx = info[2]
    for r in range(blocks):
        for j in range(OWN):
            for place, own in enumerate(own_runs(ctx, blocks * OWN)):
                @pl.when(order[r * OWN + j] == own)
                def _():
                    out_grad[:, part_slice(place)] = grads[r][:, part_slice(j)]

    total[...] = middle[...]
    back[...] = jnp.zeros_like(back)
    unit = g0.shape[1] // 3
    for sources, targets in (((b0, b1), (g0, g1)), ((b2, b3), (g2, g3))):
        feed_chunk(sources, targets, unit, normed, out_grad, total, back)


def feed_last_kernel(
    labels, info, normed, out_grad, middle_in, out_weight, weight, attended_t, total_in, back_in,
    a0, a1, a2, a3,
    hidden_out, grad_middle_out, grad_att_t, deltas, gain_grad, g0, g1, g2, g3,
    total, back, pieces,
):
    me, core = info[0], info[1]
    width = normed.shape[0]
    unit = a0.shape[1] // 3
    total[...] = total_in[...]
    back[...] = back_in[...]
    for sources, targets in (((a0, a1), (g0, g1)), ((a2, a3), (g2, g3))):
        feed_chunk(sources, targets, unit, normed, out_grad, total, back)
    hidden_out[...] = total[...].astype(bf16)
    middle = middle_in[...]
    scale = norm_scale(middle)
    unit_rows = middle * scale
    grad_normed = back[...]
    grad_unit = grad_normed * weight[:, PROJECTED + 1 : PROJECTED + 2].astype(f32)
    mean = jnp.mean(grad_unit * unit_rows, axis=0, keepdims=True)
    grad_middle = out_grad[...].astype(f32) + scale * (grad_unit - unit_rows * mean)
    grad_middle_out[...] = grad_middle
    gain_grad[...] = jnp.broadcast_to(
        jnp.sum(grad_normed * unit_rows, axis=1, keepdims=True), gain_grad.shape
    )
    low = grad_middle.astype(bf16)
    grad_att = dot(out_weight[...], low, 0, 0).astype(bf16)
    grad_att_t[...] = grad_att
    for h in range(QUERY_HEADS):
        deltas[h // GROUP, h % GROUP : h % GROUP + 1, :] = jnp.sum(
            grad_att[head_slice(h)].astype(f32) * attended_t[head_slice(h), :], axis=0, keepdims=True
        )
    grad_weight = dot(low, attended_t[...].astype(bf16), 1, 1)
    shards = pieces.shape[0]
    half = pieces.shape[1] // 2
    shard_rows = width // shards
    pieces[...] = jnp.zeros_like(pieces)
    for s in range(shards):
        pieces[s, :shard_rows, :] = grad_weight[s * shard_rows : (s + 1) * shard_rows]
    for group, own, pair in zip(labels, (g0, g1), (g2, g3)):
        for slot, label in enumerate(group):
            for target, side in ((own, core), (pair, 1 - core)):
                lines = pl.ds(pl.multiple_of(side * half, 16), half)
                target[slot, 3 * unit :, :] = pieces[me ^ label, lines, :].astype(bf16)


def attend_back_kernel(
    info, query_t, kv_t, kv_rows, grad_att_t, log_totals, deltas, cosine, sine,
    grad_query_t, grad_kv_t, kv_sums, query_sums,
):
    runs = kv_rows.shape[1] // RUN
    ctx = info[2]
    kv_sums[...] = jnp.zeros_like(kv_sums)
    for j, own in enumerate(own_runs(ctx, runs)):
        query = side_by_side(query_t, j)
        grad = side_by_side(grad_att_t, j)
        empty = jnp.zeros_like(query)
        query_deep = jnp.concatenate([query, empty], axis=0)
        grad_deep = jnp.concatenate([empty, grad], axis=0)
        query_rows = query_deep.T
        grad_rows = grad_deep.T
        here = part_slice(j)
        logs = jnp.concatenate([log_totals[0, h : h + 1, here] for h in range(GROUP)], axis=1)
        delta = jnp.concatenate([deltas[0, h : h + 1, here] for h in range(GROUP)], axis=1)

        def tile(place, masked):
            kv = kv_rows[0, place, :]
            probabilities = jnp.exp(dot(kv, query_deep, 1, 0) - logs)
            if masked:
                probabilities = jnp.where(causal(), probabilities, 0.0)
            grad_scores = probabilities * (dot(kv, grad_deep, 1, 0) - delta)
            low = grad_scores.astype(bf16)
            kv_sums[place, :] += dot(low, query_rows, 1, 0) + dot(
                probabilities.astype(bf16), grad_rows, 1, 0
            )
            return dot(kv_t[:HEAD_FEATURES, place], low, 1, 0)

        query_sums[...] = tile(run_slice(own), True)

        def advance(place, nothing):
            query_sums[...] += tile(run_slice(place), False)
            return nothing

        lax.fori_loop(0, own, advance, 0)
        cos, sin = cosine[:, run_slice(own)], sine[:, run_slice(own)]
        for h in range(GROUP):
            part = query_sums[:, part_slice(h)] * SCALE
            grad_query_t[head_slice(h), here] = rotate_back(part, cos, sin).astype(bf16)

    for label in range(runs // OWN):
        for j, run in enumerate(own_runs(ctx ^ label, runs)):
            cos, sin = cosine[:, run_slice(run)], sine[:, run_slice(run)]
            block = kv_sums[run_slice(run), :].T
            grad_kv_t[label, 0, :, part_slice(j)] = jnp.concatenate(
                [rotate_back(block[:HEAD_FEATURES], cos, sin), block[HEAD_FEATURES:]], axis=0
            ).astype(bf16)


def weight_grad_kernel(
    labels, info, grad_query_t, grad_kv_t, normed_t, weight, feed_gain, g0, g1, g2, g3, sums, pieces
):
    me, core, ctx = info[0], info[1], info[2]
    width, length = normed_t.shape
    blocks = grad_kv_t.shape[0]
    runs = length // RUN
    shards = pieces.shape[1]
    shard_rows = width // shards
    tokens = OWN * RUN

    def normed(index):
        return jnp.concatenate(
            [normed_t[:, run_slice(run)] for run in own_runs(index, runs)], axis=1
        )

    sums[:, :QUERY_WIDTH] = dot(normed(ctx), grad_query_t[...], 1, 1)
    total = dot(normed(ctx), grad_kv_t[0].reshape(KV_WIDTH, tokens), 1, 1)
    for label in range(1, blocks):
        total += dot(normed(ctx ^ label), grad_kv_t[label].reshape(KV_WIDTH, tokens), 1, 1)
    sums[:, QUERY_WIDTH:PROJECTED] = total
    products = jnp.sum(sums[:, :PROJECTED] * weight[:, :PROJECTED].astype(f32), axis=1, keepdims=True)
    sums[:, PROJECTED:] = jnp.zeros((width, PADDED - PROJECTED), f32)
    sums[:, PROJECTED : PROJECTED + 1] = products / weight[:, PROJECTED : PROJECTED + 1].astype(f32)
    sums[:, PROJECTED + 1 : PROJECTED + 2] = feed_gain[:, :1]
    for side in range(2):
        for s in range(shards):
            pieces[side, s] = sums[
                s * shard_rows : (s + 1) * shard_rows, side * PART : (side + 1) * PART
            ].astype(bf16)
    for group, own, pair in zip(labels, (g0, g1), (g2, g3)):
        for slot, label in enumerate(group):
            own[slot] = pieces[core, me ^ label]
            pair[slot] = pieces[1 - core, me ^ label]


def input_grad_kernel(grad_query_t, grad_kv_t, weight, hidden, grad_middle, input_grad):
    grads = jnp.concatenate([grad_query_t[...], grad_kv_t[...]], axis=0)
    grad_normed = dot(weight[:, :PROJECTED], grads, 1, 0)
    rows = hidden[...].astype(f32)
    scale = norm_scale(rows)
    unit_rows = rows * scale
    grad_unit = grad_normed * weight[:, PROJECTED : PROJECTED + 1].astype(f32)
    mean = jnp.mean(grad_unit * unit_rows, axis=0, keepdims=True)
    input_grad[...] = (grad_middle[...] + scale * (grad_unit - unit_rows * mean)).astype(bf16)


def give_back_kernel(blocks, info, order, *refs):
    sources, target = refs[:blocks], refs[blocks]
    ctx = info[2]
    runs = blocks * OWN
    for j in range(OWN):
        run = order[j]
        late = (run >= blocks).astype(jnp.int32)
        holder = jnp.where(run >= blocks, runs - 1 - run, run)
        for label in range(blocks):
            @pl.when((ctx ^ label) == holder)
            def _():
                target[:, part_slice(j)] = sources[label][:, run_slice(late)].astype(target.dtype)


def finish_feed_kernel(info, a_own, a_pair, b_own, b_pair, gate_g, up_g, down_g, out_g, spare):
    core = info[1]
    unit_a, unit_b = gate_g.shape[0] // 3, gate_g.shape[0] // 6
    half = spare.shape[0] // 2
    for a, b, side in ((a_own, b_own, core), (a_pair, b_pair, 1 - core)):
        for place, target in enumerate((gate_g, up_g, down_g)):
            rows = pl.ds(pl.multiple_of(side * unit_a, 8), unit_a)
            target[rows, :] = a[place * unit_a : (place + 1) * unit_a, :].astype(f32)
            rows = pl.ds(pl.multiple_of(2 * unit_a + side * unit_b, 8), unit_b)
            target[rows, :] = b[place * unit_b : (place + 1) * unit_b, :].astype(f32)
        spare[pl.ds(pl.multiple_of(side * half, 8), half), :] = a[3 * unit_a :, :].astype(f32)
    out_g[...] = spare[: out_g.shape[0], :]


def finish_projection_kernel(info, own, pair, query_g, key_g, value_g, attn_gain_g, mlp_gain_g, spare):
    core = info[1]
    for source, side in ((own, core), (pair, 1 - core)):
        spare[:, pl.ds(pl.multiple_of(side * PART, PART), PART)] = source[...].astype(f32)
    query_g[...] = spare[:, :QUERY_WIDTH]
    for g in range(KEY_VALUE_HEADS):
        start = QUERY_WIDTH + g * PAIR
        key_g[:, head_slice(g)] = spare[:, start : start + HEAD_FEATURES]
        value_g[:, head_slice(g)] = spare[:, start + HEAD_FEATURES : start + PAIR]
    attn_gain_g[...] = row_of(spare[:, PROJECTED : PROJECTED + 1])
    mlp_gain_g[...] = row_of(spare[:, PROJECTED + 1 : PROJECTED + 2])


def shape(dims, kind):
    return jax.ShapeDtypeStruct(dims, kind)


SCALARS = pl.BlockSpec(memory_space=pltpu.SMEM)


def whole(array):
    count = len(array.shape)
    return pl.BlockSpec(array.shape, lambda *step: (0,) * count)


def wholes(arrays):
    return [whole(array) for array in arrays]


def call(kernel, outputs, flops, grid=(), ins=None, outs=None, scratch=()):
    return pl.pallas_call(
        kernel,
        out_shape=outputs,
        grid=grid,
        in_specs=ins,
        out_specs=outs if outs is not None else wholes(outputs),
        scratch_shapes=scratch,
        compiler_params=pltpu.CompilerParams(vmem_limit_bytes=VMEM_BYTES),
        cost_estimate=pl.CostEstimate(flops=int(flops), bytes_accessed=0, transcendentals=0),
    )


def on_device(
    hidden_in,
    positions,
    out_grad,
    attn_gain,
    query_weight,
    key_matrix,
    value_matrix,
    out_weight,
    mlp_gain,
    gate_weight,
    up_weight,
    down_weight,
):
    hidden_t = hidden_in[0].T
    out_grad_t = out_grad[0].T
    width, tokens = hidden_t.shape
    blocks = lax.axis_size("ctx")
    shards = lax.axis_size("fsdp")
    length = blocks * tokens
    runs = blocks * OWN
    me = lax.axis_index("fsdp")
    ctx = lax.axis_index("ctx")
    shard_rows = width // shards
    ff_rows = down_weight.shape[0]
    unit_a, unit_b = ff_rows // 3, ff_rows // 6
    half = -(-shard_rows // 32) * 16
    fbits = axis_bits("fsdp")
    inner_bits = tuple(reversed(fbits[1:]))
    last_bit = fbits[0]
    ctx_bits = axis_bits("ctx")
    far_bits = tuple(reversed(ctx_bits))
    info = jnp.stack([me, ctx & 1, ctx]).astype(jnp.int32)

    groups = [[0]]
    for bit in inner_bits:
        groups[0] = groups[0] + [label ^ bit for label in groups[0]]
    groups.append([label ^ last_bit for label in groups[0]])
    slots = len(groups[0])

    def gather_step(stack, bit):
        return jnp.concatenate([stack, swap(stack, "fsdp", bit)], axis=0)

    prepare_ins = (
        hidden_t,
        positions,
        query_weight,
        key_matrix,
        value_matrix,
        attn_gain[None],
        mlp_gain[None],
        gate_weight.T,
        up_weight.T,
        down_weight,
        out_weight.T,
    )
    extended, w, a, b = call(
        prepare_kernel,
        [
            shape((width + MARK, tokens), bf16),
            shape((shard_rows, PART), bf16),
            shape((3 * unit_a, width), bf16),
            shape((3 * unit_b + half, width), bf16),
        ],
        0,
        ins=[SCALARS] + wholes(prepare_ins),
        scratch=[pltpu.VMEM((shard_rows, PADDED), f32), pltpu.VMEM((2 * half, width), f32)],
    )(info, *prepare_ins)

    frequencies = rope_base ** (-jnp.arange(HALF, dtype=f32) / HALF)
    angles = frequencies[:, None] * jnp.arange(length, dtype=jnp.int32).astype(f32)[None, :]
    cosine, sine = jnp.cos(angles), jnp.sin(angles)

    exts = gather_all(extended, far_bits)
    w, a, b = w[None], a[None], b[None]
    for bit in inner_bits:
        w = gather_step(w, bit)
    w, b = tie(w, b)
    w_stacks = [w, swap(w, "fsdp", last_bit)]
    b = gather_step(b, inner_bits[0])
    w_stacks += [swap(stack, "ctx", 1) for stack in w_stacks]
    w_stacks[1], a = tie(w_stacks[1], a)
    for bit in inner_bits[1:]:
        b = gather_step(b, bit)
    a = gather_step(a, inner_bits[0])
    exts[0], out_grad_t = tie(exts[0], out_grad_t)
    exts[-1], b, a = tie(exts[-1], b, a)

    heads_t = shape((QUERY_WIDTH, tokens), bf16)
    model_low = shape((width, tokens), bf16)
    model_wide = shape((width, tokens), f32)
    query_t, kv_t, kv_rows, normed_t, weight, hidden_own, order = call(
        functools.partial(project_kernel, blocks, groups),
        [
            heads_t,
            shape((KV_WIDTH, length), bf16),
            shape((KEY_VALUE_HEADS, length, PAIR), bf16),
            shape((width, length), bf16),
            shape((width, PADDED), bf16),
            model_low,
            shape((runs,), jnp.int32),
        ],
        2 * width * (tokens * QUERY_WIDTH + length * KV_WIDTH),
        grid=(blocks,),
        ins=[SCALARS] + wholes(exts) + wholes(w_stacks) + wholes((cosine, sine)),
        outs=[
            whole(heads_t),
            pl.BlockSpec((KV_WIDTH, tokens), lambda r: (0, r)),
            pl.BlockSpec((KEY_VALUE_HEADS, tokens, PAIR), lambda r: (0, r, 0)),
            pl.BlockSpec((width, tokens), lambda r: (0, r)),
            pl.BlockSpec((width, PADDED), lambda r: (0, 0)),
            whole(model_low),
            SCALARS,
        ],
        scratch=[
            pltpu.VMEM((runs, width, RUN), bf16),
            pltpu.VMEM((PADDED, width), bf16),
            pltpu.VMEM((2, shards, shard_rows, PART), bf16),
        ],
    )(info, *exts, *w_stacks, cosine, sine)

    grads_in = gather_all(out_grad_t, far_bits)
    b_stacks = [b, swap(b, "fsdp", last_bit)]
    for bit in inner_bits[1:]:
        a = gather_step(a, bit)

    group_rows = pl.BlockSpec((GROUP * HEAD_FEATURES, tokens), lambda g: (g, 0))
    group_kv_t = pl.BlockSpec((PAIR, length), lambda g: (g, 0))
    group_kv = pl.BlockSpec((1, length, PAIR), lambda g: (g, 0, 0))
    group_line = pl.BlockSpec((1, GROUP, tokens), lambda g: (g, 0, 0))
    lines = shape((KEY_VALUE_HEADS, GROUP, tokens), f32)
    query_t, a = tie(query_t, a)
    attended_t, log_totals = call(
        attend_kernel,
        [shape((QUERY_WIDTH, tokens), f32), lines],
        4 * 4 * tokens * length * QUERY_WIDTH,
        grid=(KEY_VALUE_HEADS,),
        ins=[SCALARS, group_rows, group_kv_t, group_kv],
        outs=[group_rows, group_line],
        scratch=[
            pltpu.VMEM((1, GROUP * RUN), f32),
            pltpu.VMEM((1, GROUP * RUN), f32),
            pltpu.VMEM((HEAD_FEATURES, GROUP * RUN), f32),
        ],
    )(info, query_t, kv_t, kv_rows)

    b_stacks += [swap(stack, "ctx", 1) for stack in b_stacks]
    a_stacks = [a, swap(a, "fsdp", last_bit)]
    square = shape((width, QUERY_WIDTH), bf16)
    middle_ins = (hidden_own, attended_t, weight, *b_stacks)
    middle, normed_mlp, full_out = call(
        functools.partial(middle_kernel, groups),
        [model_wide, model_low, square],
        2 * tokens * width * QUERY_WIDTH,
        ins=[SCALARS] + wholes(middle_ins),
        scratch=[pltpu.VMEM((2, shards, half, width), bf16)],
    )(info, *middle_ins)

    first_ins = (*grads_in, normed_mlp, middle, *b_stacks)
    grad_stack_b = shape((slots, 3 * unit_b, width), bf16)
    out_grad_own, total, back, *gb = call(
        functools.partial(feed_first_kernel, blocks),
        [model_low, model_wide, model_wide] + [grad_stack_b] * 4,
        6 * tokens * width * ff_rows * shards,
        ins=[SCALARS, SCALARS] + wholes(first_ins),
    )(info, order, *first_ins)

    a_stacks += [swap(stack, "ctx", 1) for stack in a_stacks]
    last_ins = (
        normed_mlp, out_grad_own, middle, full_out, weight, attended_t, total, back, *a_stacks,
    )
    grad_stack_a = shape((slots, 3 * unit_a + half, width), bf16)
    hidden_own_out, grad_middle, grad_att_t, deltas, feed_gain, *ga = call(
        functools.partial(feed_last_kernel, groups),
        [model_low, model_wide, heads_t, lines, shape((width, 128), f32)] + [grad_stack_a] * 4,
        12 * tokens * width * ff_rows * shards,
        ins=[SCALARS] + wholes(last_ins),
        scratch=[
            pltpu.VMEM((width, tokens), f32),
            pltpu.VMEM((width, tokens), f32),
            pltpu.VMEM((shards, 2 * half, width), f32),
        ],
    )(info, *last_ins)

    def cross_core(stacks):
        return [add_low(stacks[i], swap(stacks[2 + i], "ctx", 1)) for i in range(2)]

    def scatter_first(stacks):
        return add_low(stacks[0], swap(stacks[1], "fsdp", last_bit))

    def scatter_step(stack, bit):
        count = stack.shape[0] // 2
        return add_low(stack[:count], swap(stack[count:], "fsdp", bit))

    def scatter_rest(stack):
        for bit in reversed(inner_bits):
            stack = scatter_step(stack, bit)
        value = stack[0]
        for bit in ctx_bits[1:]:
            value = add_low(value, swap(value, "ctx", bit))
        return value, swap(value, "ctx", 1)

    gb = cross_core(gb)
    grad_att_t, gb[1] = tie(grad_att_t, gb[1])
    grad_kv_shape = shape((blocks, KEY_VALUE_HEADS, PAIR, tokens), bf16)
    grad_query_t, grad_kv_t = call(
        attend_back_kernel,
        [heads_t, grad_kv_shape],
        10 * 4 * tokens * length * QUERY_WIDTH,
        grid=(KEY_VALUE_HEADS,),
        ins=[SCALARS, group_rows, group_kv_t, group_kv, group_rows, group_line, group_line]
        + [whole(cosine), whole(sine)],
        outs=[
            group_rows,
            pl.BlockSpec((blocks, 1, PAIR, tokens), lambda g: (0, g, 0, 0)),
        ],
        scratch=[
            pltpu.VMEM((length, PAIR), f32),
            pltpu.VMEM((HEAD_FEATURES, GROUP * RUN), f32),
        ],
    )(info, query_t, kv_t, kv_rows, grad_att_t, log_totals, deltas, cosine, sine)
    ga = cross_core(ga)
    gb = scatter_first(gb)
    outs_low = gather_all(hidden_own_out, far_bits)
    grad_query_t, ga[1], gb = tie(grad_query_t, ga[1], gb)

    grad_stack_w = shape((slots, shard_rows, PART), bf16)
    grad_ins = (grad_query_t, grad_kv_t, normed_t, weight, feed_gain)
    gw = call(
        functools.partial(weight_grad_kernel, groups),
        [grad_stack_w] * 4,
        2 * width * (tokens * QUERY_WIDTH + length * KV_WIDTH),
        ins=[SCALARS] + wholes(grad_ins),
        scratch=[
            pltpu.VMEM((width, PADDED), f32),
            pltpu.VMEM((2, shards, shard_rows, PART), bf16),
        ],
    )(info, *grad_ins)

    own_kv = grad_kv_t
    for bit in ctx_bits:
        pairs = own_kv.reshape((own_kv.shape[0] // 2, 2) + own_kv.shape[1:])
        own_kv = add_low(pairs[:, 0], swap(pairs[:, 1], "ctx", bit))
    own_kv = own_kv.reshape(KV_WIDTH, tokens)
    end_ins = (grad_query_t, own_kv, weight, hidden_own, grad_middle)
    (input_grad_own,) = call(
        input_grad_kernel,
        [model_low],
        2 * tokens * width * PROJECTED,
        ins=wholes(end_ins),
    )(*end_ins)

    w_own, w_pair = scatter_rest(scatter_first(cross_core(gw)))
    b_own, b_pair = scatter_rest(gb)
    a_own, a_pair = scatter_rest(scatter_first(ga))
    input_grads = gather_all(input_grad_own, far_bits)

    def give_back(pieces, kind):
        (result,) = call(
            functools.partial(give_back_kernel, blocks),
            [shape((width, tokens), kind)],
            0,
            ins=[SCALARS, SCALARS] + wholes(pieces),
        )(info, order, *pieces)
        return result.T[None]

    ff_grad = shape((ff_rows, width), f32)
    gate_g, up_g, down_g, out_g = call(
        finish_feed_kernel,
        [ff_grad, ff_grad, ff_grad, shape((shard_rows, width), f32)],
        0,
        ins=[SCALARS] + wholes((a_own, a_pair, b_own, b_pair)),
        scratch=[pltpu.VMEM((2 * half, width), f32)],
    )(info, a_own, a_pair, b_own, b_pair)
    kv_grad = shape((shard_rows, KV_WIDTH // 2), f32)
    gain_line = shape((1, shard_rows), f32)
    query_g, key_g, value_g, attn_gain_g, mlp_gain_g = call(
        finish_projection_kernel,
        [shape((shard_rows, QUERY_WIDTH), f32), kv_grad, kv_grad, gain_line, gain_line],
        0,
        ins=[SCALARS] + wholes((w_own, w_pair)),
        scratch=[pltpu.VMEM((shard_rows, PADDED), f32)],
    )(info, w_own, w_pair)

    return (
        give_back(outs_low, bf16),
        give_back(input_grads, f32),
        attn_gain_g[0],
        query_g,
        key_g,
        value_g,
        out_g.T,
        mlp_gain_g[0],
        gate_g.T,
        up_g.T,
        down_g,
    )


def solution(mesh):
    placed = (
        P("fsdp", "ctx", None),
        P("fsdp", "ctx"),
        P("fsdp", "ctx", None),
        P("fsdp"),
        P("fsdp", None),
        P("fsdp", None),
        P("fsdp", None),
        P(None, "fsdp"),
        P("fsdp"),
        P(None, "fsdp"),
        P(None, "fsdp"),
        P("fsdp", None),
    )
    return jax.shard_map(
        on_device,
        mesh=mesh,
        in_specs=placed,
        out_specs=(
            P("fsdp", "ctx", None),
            P("fsdp", "ctx", None),
            P("fsdp"),
            P("fsdp", None),
            P("fsdp", None),
            P("fsdp", None),
            P(None, "fsdp"),
            P("fsdp"),
            P(None, "fsdp"),
            P(None, "fsdp"),
            P("fsdp", None),
        ),
        check_vma=False,
    )
```

time: 300 us -> 255 us (0.85)
  waiting for transfers between devices: 103 us -> 66.8 us
  Pallas kernels: 67.5 us -> 97 us
  other arithmetic: 36.6 us -> 18.4 us
  starting transfers between devices: 68 us -> 50.2 us
  local copies, waits for them, and re-layouts: 23.8 us -> 20.2 us
    ppermute x35 -> x50, waiting for transfers between devices: 103 us -> 66.8 us  [swap(): lax.ppermute(value, axis, [(source, source ^ bit) for source in range(cou...]
    pallas_call x6 -> x12, Pallas kernels: 58.4 us -> 79.6 us  [the longest x1 19.8 us: on_device(): call(attend_back_kernel, [heads_t, grad_kv_shape], 10 * 4 * tokens * leng...]
    ppermute x35 -> x50, starting transfers between devices: 68 us -> 50.2 us  [swap(): lax.ppermute(value, axis, [(source, source ^ bit) for source in range(cou...]
    pallas_call x1, Pallas kernels: 9.08 us -> 17.4 us  [on_device(): call(attend_kernel, [shape((QUERY_WIDTH, tokens), f32), lines], 4 * 4 * t...]
    concatenate x13 -> x6, other arithmetic: 11.9 us -> 4.16 us  [gather_step(): return jnp.concatenate([stack, swap(stack, 'fsdp', bit)], axis=0)]
    slice x19 -> x7, local copies, waits for them, and re-layouts: 9.2 us -> 1.89 us  [scatter_step(): return add_low(stack[:count], swap(stack[count:], 'fsdp', bit))]
    ppermute x0 -> x4, local copies, waits for them, and re-layouts: none -> 6.01 us  [swap(): lax.ppermute(value, axis, [(source, source ^ bit) for source in range(cou...]
    unnamed x28 -> x58, local copies, waits for them, and re-layouts: 11.5 us -> 5.58 us
  transfers between devices with their start and end apart: 35 -> 50, of which waited for: 16 -> 13; matrix products, arithmetic and copies ran while one was open for 17% -> 13% of each run, Pallas kernels for 9% -> 36%
where the time goes in v2:
time: 255 us; the launch traced here: 254 us
  Pallas kernels  97 us (38%)
  waiting for transfers between devices  66.8 us (26%)
  starting transfers between devices  50.2 us (20%)
  local copies, waits for them, and re-layouts  20.2 us (8%)
  other arithmetic  18.4 us (7%)
    ppermute x50, waiting for transfers between devices, swap(): lax.ppermute(value, axis, [(source, source ^ bit) for source in range(cou...  66.8 us
    ppermute x50, starting transfers between devices, swap(): lax.ppermute(value, axis, [(source, source ^ bit) for source in range(cou...  50.2 us
    pallas_call x1, Pallas kernels, on_device(): call(attend_back_kernel, [heads_t, grad_kv_shape], 10 * 4 * tokens * leng...  19.8 us
    pallas_call x1, Pallas kernels, on_device(): call(attend_kernel, [shape((QUERY_WIDTH, tokens), f32), lines], 4 * 4 * t...  17.4 us
    pallas_call x1, Pallas kernels, on_device(): call(functools.partial(feed_last_kernel, groups), [model_low, model_wide,...  15.8 us
    convert_element_type x13, other arithmetic, add_low(): return (left.astype(f32) + right.astype(f32)).astype(bf16)  10.3 us
    pallas_call x1, Pallas kernels, on_device(): call(functools.partial(project_kernel, blocks, groups), [heads_t, shape((...  8.37 us
    pallas_call x1, Pallas kernels, on_device(): call(functools.partial(feed_first_kernel, blocks), [model_low, model_wide...  8.21 us
  transfers between devices with their start and end apart: 50, of which 13 were waited for; matrix products, arithmetic and copies ran while one was open for 13% of the time, Pallas kernels for 36%

profile of v2, /device:TPU:0, one launch (start us, length us, event | category | flops | bytes accessed | tf_op | source)
XLA Modules:
  0.0 253.8 jit_solution(10952972467194096796)
XLA Ops:
  1.3 2.6 %shard_map.203 = (bf16[592,512]{1,0:T(8,128)(2,1)}, bf16[72,512]{1,0:T(8,128)(2,1)}, bf16[192,576]{1,0:T(8,128)(2,1)}, bf16[144,576]{1,0:T(8,128)(2,1)}) custom-call(s32[3]{0:T(128)} %pad_add_fusion.info, bf16[576,512]{1,0:T(8,128)(2,1)} %bitcast.63, s32[1,512]{1,0:T(1,128)} %positions.1, bf16[72,576]{1,0:T(8,128)(2,1)} %query_w.1, bf16[72,192]{1,0:T(8,128)(2,1)} %key_w.1, ...), custom_call_target="tpu_custom_call" | custom-call | tf_op jit(solution)/shard_map/pallas_call | solution.py:598
  3.9 4.1 %collective-permute-start.3 = (bf16[1,72,512]{2,1,0:T(8,128)(2,1)}, bf16[1,72,512]{2,1,0:T(8,128)(2,1)S(1)}, u32[]{:S(2)}, u32[]{:S(2)}) collective-permute-start(bf16[1,72,512]{2,1,0:T(8,128)(2,1)} %bitcast.65), channel_id=1, source_target_pairs={{0,4},{1,5},{2,6},{3,7},{4,0},{5,1},{6,2},{7,3},{8,12},{9,13},{10,... | collective-permute-start | bytes 221192 | tf_op jit(solution)/shard_map/ppermute | solution.py:43
  9.4 2.6 %collective-permute-done.3 = bf16[1,72,512]{2,1,0:T(8,128)(2,1)S(1)} collective-permute-done((bf16[1,72,512]{2,1,0:T(8,128)(2,1)}, bf16[1,72,512]{2,1,0:T(8,128)(2,1)S(1)}, u32[]{:S(2)}, u32[]{:S(2)}) %collective-permute-start.3) | collective-permute-done | bytes 73760 | tf_op jit(solution)/shard_map/ppermute | solution.py:43
  13.8 4.4 %collective-permute-done.4 = bf16[2,72,512]{2,1,0:T(8,128)(2,1)S(1)} collective-permute-done((bf16[2,72,512]{2,1,0:T(8,128)(2,1)S(1)}, bf16[2,72,512]{2,1,0:T(8,128)(2,1)S(1)}, u32[]{:S(2)}, u32[]{:S(2)}) %collective-permute-start.4) | collective-permute-done | bytes 147488 | tf_op jit(solution)/shard_map/ppermute | solution.py:43
  19.1 2.7 %collective-permute-start.5 = (bf16[1,144,576]{2,1,0:T(8,128)(2,1)}, bf16[1,144,576]{2,1,0:T(8,128)(2,1)S(1)}, u32[]{:S(2)}, u32[]{:S(2)}) collective-permute-start(bf16[1,144,576]{2,1,0:T(8,128)(2,1)} %bitcast.60), channel_id=1, source_target_pairs={{0,4},{1,5},{2,6},{3,7},{4,0},{5,1},{6,2},{7,3},{8,12},{9,13},{10,... | collective-permute-start | bytes 497672 | tf_op jit(solution)/shard_map/ppermute | solution.py:43
  23.4 6.6 %collective-permute-done.5 = bf16[1,144,576]{2,1,0:T(8,128)(2,1)S(1)} collective-permute-done((bf16[1,144,576]{2,1,0:T(8,128)(2,1)}, bf16[1,144,576]{2,1,0:T(8,128)(2,1)S(1)}, u32[]{:S(2)}, u32[]{:S(2)}) %collective-permute-start.5) | collective-permute-done | bytes 165920 | tf_op jit(solution)/shard_map/ppermute | solution.py:43
  32.3 3.3 %collective-permute-start.8 = (bf16[1,192,576]{2,1,0:T(8,128)(2,1)S(1)}, bf16[1,192,576]{2,1,0:T(8,128)(2,1)S(1)}, u32[]{:S(2)}, u32[]{:S(2)}) collective-permute-start(bf16[1,192,576]{2,1,0:T(8,128)(2,1)S(1)} %bitcast.70), channel_id=1, source_target_pairs={{0,4},{1,5},{2,6},{3,7},{4,0},{5,1},{6,2},{7,3},{8,12},{9,13},{10,... | collective-permute-start | bytes 663560 | tf_op jit(solution)/shard_map/ppermute | solution.py:43
  35.7 10.2 %collective-permute-done.6 = bf16[2,144,576]{2,1,0:T(8,128)(2,1)S(1)} collective-permute-done((bf16[2,144,576]{2,1,0:T(8,128)(2,1)S(1)}, bf16[2,144,576]{2,1,0:T(8,128)(2,1)S(1)}, u32[]{:S(2)}, u32[]{:S(2)}) %collective-permute-start.6) | collective-permute-done | bytes 331808 | tf_op jit(solution)/shard_map/ppermute | solution.py:43
  52.6 7.0 %collective-permute-done.16.refs_2_ = bf16[576,512]{1,0:T(8,128)(2,1)} collective-permute-done((bf16[576,512]{1,0:T(8,128)(2,1)}, bf16[576,512]{1,0:T(8,128)(2,1)}, u32[]{:S(2)}, u32[]{:S(2)}) %collective-permute-start.16) | collective-permute-done | bytes 589856 | tf_op jit(solution)/shard_map/ppermute | solution.py:43
  60.9 8.4 %shard_map.204 = (bf16[576,512]{1,0:T(8,128)(2,1)}, bf16[384,2048]{1,0:T(8,128)(2,1)}, bf16[3,2048,128]{2,1,0:T(8,128)(2,1)}, bf16[576,2048]{1,0:T(8,128)(2,1)},...) custom-call(s32[3]{0:T(128)} %pad_add_fusion.info, bf16[592,512]{1,0:T(8,128)(2,1)} %get-tuple-element.75.refs_0_, ...), custom_call_target="tpu_custom_call" | custom-call | flops 1245708288 | tf_op jit(solution)/shard_map/pallas_call | solution.py:633
  72.1 17.4 %shard_map.205 = (f32[576,512]{1,0:T(8,128)}, f32[3,3,512]{2,1,0:T(4,128)}) custom-call(s32[3]{0:T(128)} %pad_add_fusion.info, bf16[576,512]{1,0:T(8,128)(2,1)} %get-tuple-element.88.query_t, bf16[384,2048]{1,0:T(8,128)(2,1)} %get-tuple-element.89.kv_t, bf16[3,2048,128]{2,1,0:T(8,128)(2,1)} %get-tuple-element.90.kv_rows), custom_call_target="tpu_custom_call" | custom-call | flops 9663676416 | tf_op jit(solution)/shard_map/pallas_call | solution.py:674
  90.4 4.8 %shard_map.206 = (f32[576,512]{1,0:T(8,128)}, bf16[576,512]{1,0:T(8,128)(2,1)}, bf16[576,576]{1,0:T(8,128)(2,1)}) custom-call(s32[3]{0:T(128)} %pad_add_fusion.info, bf16[576,512]{1,0:T(8,128)(2,1)} %get-tuple-element.85.hidden, f32[576,512]{1,0:T(8,128)} %get-tuple-element.91.attended_t, bf16[576,1024]{1,0:T(8,128)(2,1)} %get-tuple-element.92.weight, ...), custom_call_target="tpu_custom_call" | custom-call | flops 339738624 | tf_op jit(solution)/shard_map/pallas_call | solution.py:692
  95.5 8.2 %shard_map.207 = (bf16[576,512]{1,0:T(8,128)(2,1)}, f32[576,512]{1,0:T(8,128)}, f32[576,512]{1,0:T(8,128)}, bf16[4,96,576]{2,1,0:T(8,128)(2,1)}, bf16[4,96,576]{...) custom-call(s32[3]{0:T(128)} %pad_add_fusion.info, s32[8]{0:T(128)} %get-tuple-element.84.order, ...), custom_call_target="tpu_custom_call" | custom-call | flops 2717908992 | tf_op jit(solution)/shard_map/pallas_call | solution.py:702
  108.0 15.8 %shard_map.208 = (bf16[576,512]{1,0:T(8,128)(2,1)}, f32[576,512]{1,0:T(8,128)}, bf16[576,512]{1,0:T(8,128)(2,1)}, f32[3,3,512]{2,1,0:T(4,128)}, f32[576,128]{1,0...) custom-call(s32[3]{0:T(128)} %pad_add_fusion.info, ...), custom_call_target="tpu_custom_call" | custom-call | flops 5435817984 | tf_op jit(solution)/shard_map/pallas_call | solution.py:714
  126.1 19.8 %shard_map.210 = (bf16[576,512]{1,0:T(8,128)(2,1)}, bf16[4,3,128,512]{3,2,1,0:T(8,128)(2,1)}) custom-call(s32[3]{0:T(128)} %pad_add_fusion.info, bf16[576,512]{1,0:T(8,128)(2,1)} %get-tuple-element.88.query_t, bf16[384,2048]{1,0:T(8,128)(2,1)} %get-tuple-element.89.kv_t, bf16[3,2048,128]{2,1,0:T(8,128)(2,1)} %get-tuple-element.90.kv_rows, ...), custom_call_target="tpu_custom_call" | custom-call | flops 24159191040 | tf_op jit(solution)/shard_map/pallas_call | solution.py:747
  162.4 6.5 %shard_map.213 = (bf16[4,72,512]{2,1,0:T(8,128)(2,1)}, bf16[4,72,512]{2,1,0:T(8,128)(2,1)}, bf16[4,72,512]{2,1,0:T(8,128)(2,1)}, bf16[4,72,512]{2,1,0:T(8,128)(2,1)}) custom-call(s32[3]{0:T(128)} %pad_add_fusion.info, bf16[576,512]{1,0:T(8,128)(2,1)} %get-tuple-element.115.grad_query_t, bf16[4,3,128,512]{3,2,1,0:T(8,128)(2,1)} %get-tuple-element.116.grad_kv_t, ...), custom_call_target="tpu_custom_call" | custom-call | flops 1245708288 | tf_op jit(solution)/shard_map/pallas_call | solution.py:770
  172.5 13.0 %collective-permute-done.41 = bf16[4,240,576]{1,2,0:T(8,128)(2,1)} collective-permute-done((bf16[4,240,576]{1,2,0:T(8,128)(2,1)}, bf16[4,240,576]{1,2,0:T(8,128)(2,1)}, u32[]{:S(2)}, u32[]{:S(2)}) %collective-permute-start.41) | collective-permute-done | bytes 1105952 | tf_op jit(solution)/shard_map/ppermute | solution.py:43
  192.7 4.2 %shard_map.211.refs_0_ = bf16[576,512]{1,0:T(8,128)(2,1)} custom-call(bf16[576,512]{1,0:T(8,128)(2,1)} %get-tuple-element.115.grad_query_t, bf16[384,512]{1,0:T(8,128)(2,1)} %bitcast.58, bf16[576,1024]{1,0:T(8,128)(2,1)} %get-tuple-element.92.weight, bf16[576,512]{1,0:T(8,128)(2,1)} %get-tuple-element.85.hidden, f32[576,512]{1,0:T(8,128)} %get-tuple-element.117.grad_middle), custom_call_target="tpu_custom_call" | custom-call | flops 566231040 | tf_op jit(solution)/shard_map/pallas_call | solution.py:787
  200.0 5.9 %collective-permute-start.47 = (bf16[1,96,576]{2,1,0:T(8,128)(2,1)S(1)}, bf16[1,96,576]{2,1,0:T(8,128)(2,1)S(1)}, u32[]{:S(2)}, u32[]{:S(2)}) collective-permute-start(bf16[1,96,576]{2,1,0:T(8,128)(2,1)S(1)} %slice.77), channel_id=1, source_target_pairs={{0,4},{1,5},{2,6},{3,7},{4,0},{5,1},{6,2},{7,3},{8,12},{9,13},{10,... | collective-permute-start | bytes 331784 | tf_op jit(solution)/shard_map/ppermute | solution.py:43
  210.0 5.2 %collective-permute-start.43 = (bf16[1,240,576]{2,1,0:T(8,128)(2,1)S(1)}, bf16[1,240,576]{2,1,0:T(8,128)(2,1)S(1)}, u32[]{:S(2)}, u32[]{:S(2)}) collective-permute-start(bf16[1,240,576]{2,1,0:T(8,128)(2,1)S(1)} %slice.75), channel_id=1, source_target_pairs={{0,4},{1,5},{2,6},{3,7},{4,0},{5,1},{6,2},{7,3},{8,12},{9,13},{10,... | collective-permute-start | bytes 829448 | tf_op jit(solution)/shard_map/ppermute | solution.py:43
  216.9 9.5 %collective-permute-done.43 = bf16[1,240,576]{2,1,0:T(8,128)(2,1)S(1)} collective-permute-done((bf16[1,240,576]{2,1,0:T(8,128)(2,1)S(1)}, bf16[1,240,576]{2,1,0:T(8,128)(2,1)S(1)}, u32[]{:S(2)}, u32[]{:S(2)}) %collective-permute-start.43) | collective-permute-done | bytes 276512 | tf_op jit(solution)/shard_map/ppermute | solution.py:43
  226.5 3.0 %collective-permute-start.44 = (bf16[240,576]{1,0:T(8,128)(2,1)S(1)}, bf16[240,576]{1,0:T(8,128)(2,1)S(1)}, u32[]{:S(2)}, u32[]{:S(2)}) collective-permute-start(bf16[240,576]{1,0:T(8,128)(2,1)S(1)} %fusion.3), channel_id=1, source_target_pairs={{0,16},{8,24},{16,0},{24,8},{1,17},{9,25},{17,1},{25,9},{2,18},{10... | collective-permute-start | bytes 829448 | tf_op jit(solution)/shard_map/ppermute | solution.py:43
  232.0 3.8 %collective-permute-done.44 = bf16[240,576]{1,0:T(8,128)(2,1)S(1)} collective-permute-done((bf16[240,576]{1,0:T(8,128)(2,1)S(1)}, bf16[240,576]{1,0:T(8,128)(2,1)S(1)}, u32[]{:S(2)}, u32[]{:S(2)}) %collective-permute-start.44) | collective-permute-done | bytes 276512 | tf_op jit(solution)/shard_map/ppermute | solution.py:43
  247.3 2.8 %shard_map.212 = f32[576,512]{1,0:T(8,128)} custom-call(s32[3]{0:T(128)} %pad_add_fusion.info, s32[8]{0:T(128)} %get-tuple-element.84.order, bf16[576,512]{1,0:T(8,128)(2,1)} %shard_map.211.refs_0_, bf16[576,512]{1,0:T(8,128)(2,1)} %copy-done.11, bf16[576,512]{1,0:T(8,128)(2,1)} %collective-permute-done.31.refs_2_, bf16[576,512]{1,0:T(8,128)(2,1)} %copy-done.12), custom_call_target="tpu_custom_call" | custom-call | tf_op jit(solution)/shard_map/pallas_call | solution.py:800
  (190 shorter events, 80.8 us)
Async XLA Ops:
  23.4 24.4 %collective-permute-start.2 = (bf16[592,512]{1,0:T(8,128)(2,1)S(1)}, bf16[592,512]{1,0:T(8,128)(2,1)S(1)}, u32[]{:S(2)}, u32[]{:S(2)}) collective-permute-start(bf16[592,512]{1,0:T(8,128)(2,1)S(1)} %collective-permute-done.1.refs_2_), channel_id=1, source_target_pairs={{0,8},{8,0},{16,24},{24,16},{1,9},{9,1},{17,25},{25,17},{2,10},{10... | collective-permute-start | bytes 1818632 | tf_op jit(solution)/shard_map/ppermute | solution.py:43
  31.8 27.8 %collective-permute-start = (bf16[592,512]{1,0:T(8,128)(2,1)S(1)}, bf16[592,512]{1,0:T(8,128)(2,1)S(1)}, u32[]{:S(2)}, u32[]{:S(2)}) collective-permute-start(bf16[592,512]{1,0:T(8,128)(2,1)S(1)} %copy-done.24), channel_id=1, source_target_pairs={{0,8},{8,0},{16,24},{24,16},{1,9},{9,1},{17,25},{25,17},{2,10},{10... | collective-permute-start | bytes 1818632 | tf_op jit(solution)/shard_map/ppermute | solution.py:43
  31.8 17.5 %collective-permute-start.9 = (bf16[4,72,512]{2,1,0:T(8,128)(2,1)S(1)}, bf16[4,72,512]{2,1,0:T(8,128)(2,1)}, u32[]{:S(2)}, u32[]{:S(2)}) collective-permute-start(bf16[4,72,512]{2,1,0:T(8,128)(2,1)S(1)} %pad_maximum_fusion.4.refs_4_), channel_id=1, source_target_pairs={{0,8},{8,0},{16,24},{24,16},{1,9},{9,1},{17,25},{25,17},{2,10},{10... | collective-permute-start | bytes 884744 | tf_op jit(solution)/shard_map/ppermute | solution.py:43
  47.7 21.6 %collective-permute-start.11 = (bf16[2,192,576]{2,1,0:T(8,128)(2,1)S(1)}, bf16[2,192,576]{2,1,0:T(8,128)(2,1)}, u32[]{:S(2)}, u32[]{:S(2)}) collective-permute-start(bf16[2,192,576]{2,1,0:T(8,128)(2,1)S(1)} %pad_maximum_fusion.2), channel_id=1, source_target_pairs={{0,2},{1,3},{2,0},{3,1},{4,6},{5,7},{6,4},{7,5},{8,10},{9,11},{10,... | collective-permute-start | bytes 1327112 | tf_op jit(solution)/shard_map/ppermute | solution.py:43
  49.3 22.8 %collective-permute-start.12 = (bf16[4,144,576]{2,1,0:T(8,128)(2,1)S(1)}, bf16[4,144,576]{2,1,0:T(8,128)(2,1)S(1)}, u32[]{:S(2)}, u32[]{:S(2)}) collective-permute-start(bf16[4,144,576]{2,1,0:T(8,128)(2,1)S(1)} %pad_maximum_fusion.1.b0.refs_6_), channel_id=1, source_target_pairs={{0,1},{1,0},{2,3},{3,2},{4,5},{5,4},{6,7},{7,6},{8,9},{9,8},{10,11... | collective-permute-start | bytes 1990664 | tf_op jit(solution)/shard_map/ppermute | solution.py:43
  59.6 35.9 %collective-permute-start.15 = (bf16[576,512]{1,0:T(8,128)(2,1)}, bf16[576,512]{1,0:T(8,128)(2,1)}, u32[]{:S(2)}, u32[]{:S(2)}) collective-permute-start(bf16[576,512]{1,0:T(8,128)(2,1)} %bitcast.11.refs_0_), channel_id=1, source_target_pairs={{0,8},{8,0},{16,24},{24,16},{1,9},{9,1},{17,25},{25,17},{2,10},{10... | collective-permute-start | bytes 1769480 | tf_op jit(solution)/shard_map/ppermute | solution.py:43
  59.6 35.9 %collective-permute-start.17 = (bf16[576,512]{1,0:T(8,128)(2,1)}, bf16[576,512]{1,0:T(8,128)(2,1)}, u32[]{:S(2)}, u32[]{:S(2)}) collective-permute-start(bf16[576,512]{1,0:T(8,128)(2,1)} %collective-permute-done.16.refs_2_), channel_id=1, source_target_pairs={{0,8},{8,0},{16,24},{24,16},{1,9},{9,1},{17,25},{25,17},{2,10},{10... | collective-permute-start | bytes 1769480 | tf_op jit(solution)/shard_map/ppermute | solution.py:43
  60.4 29.1 %collective-permute-start.13 = (bf16[4,144,576]{2,1,0:T(8,128)(2,1)S(1)}, bf16[4,144,576]{2,1,0:T(8,128)(2,1)S(1)}, u32[]{:S(2)}, u32[]{:S(2)}) collective-permute-start(bf16[4,144,576]{2,1,0:T(8,128)(2,1)S(1)} %pad_maximum_fusion.1.b0.refs_6_), channel_id=1, source_target_pairs={{0,8},{8,0},{16,24},{24,16},{1,9},{9,1},{17,25},{25,17},{2,10},{10... | collective-permute-start | bytes 1990664 | tf_op jit(solution)/shard_map/ppermute | solution.py:43
  70.5 24.7 %collective-permute-start.18 = (bf16[4,192,576]{2,1,0:T(8,128)(2,1)S(1)}, bf16[4,192,576]{2,1,0:T(8,128)(2,1)}, u32[]{:S(2)}, u32[]{:S(2)}) collective-permute-start(bf16[4,192,576]{2,1,0:T(8,128)(2,1)S(1)} %pad_maximum_fusion.a0), channel_id=1, source_target_pairs={{0,1},{1,0},{2,3},{3,2},{4,5},{5,4},{6,7},{7,6},{8,9},{9,8},{10,11... | collective-permute-start | bytes 2654216 | tf_op jit(solution)/shard_map/ppermute | solution.py:43
  72.1 17.8 %collective-permute-start.14 = (bf16[4,144,576]{2,1,0:T(8,128)(2,1)S(1)}, bf16[4,144,576]{2,1,0:T(8,128)(2,1)}, u32[]{:S(2)}, u32[]{:S(2)}) collective-permute-start(bf16[4,144,576]{2,1,0:T(8,128)(2,1)S(1)} %collective-permute-done.12.b1.refs_7_), channel_id=1, source_target_pairs={{0,8},{8,0},{16,24},{24,16},{1,9},{9,1},{17,25},{25,17},{2,10},{10... | collective-permute-start | bytes 1990664 | tf_op jit(solution)/shard_map/ppermute | solution.py:43
  89.5 17.4 %collective-permute-start.19 = (bf16[4,192,576]{2,1,0:T(8,128)(2,1)S(1)}, bf16[4,192,576]{2,1,0:T(8,128)(2,1)S(1)}, u32[]{:S(2)}, u32[]{:S(2)}) collective-permute-start(bf16[4,192,576]{2,1,0:T(8,128)(2,1)S(1)} %pad_maximum_fusion.a0), channel_id=1, source_target_pairs={{0,8},{8,0},{16,24},{24,16},{1,9},{9,1},{17,25},{25,17},{2,10},{10... | collective-permute-start | bytes 2654216 | tf_op jit(solution)/shard_map/ppermute | solution.py:43
  103.9 46.2 %collective-permute-start.26 = (bf16[4,96,576]{2,1,0:T(8,128)(2,1)}, bf16[4,96,576]{2,1,0:T(8,128)(2,1)}, u32[]{:S(2)}, u32[]{:S(2)}) collective-permute-start(bf16[4,96,576]{2,1,0:T(8,128)(2,1)} %get-tuple-element.113), channel_id=1, source_target_pairs={{0,8},{8,0},{16,24},{24,16},{1,9},{9,1},{17,25},{25,17},{2,10},{10... | collective-permute-start | bytes 1327112 | tf_op jit(solution)/shard_map/ppermute | solution.py:43
  123.8 26.3 %collective-permute-start.27 = (bf16[4,96,576]{2,1,0:T(8,128)(2,1)S(1)}, bf16[4,96,576]{2,1,0:T(8,128)(2,1)}, u32[]{:S(2)}, u32[]{:S(2)}) collective-permute-start(bf16[4,96,576]{2,1,0:T(8,128)(2,1)S(1)} %add_convert_fusion.6), channel_id=1, source_target_pairs={{0,1},{1,0},{2,3},{3,2},{4,5},{5,4},{6,7},{7,6},{8,9},{9,8},{10,11... | collective-permute-start | bytes 1327112 | tf_op jit(solution)/shard_map/ppermute | solution.py:43
  125.9 26.3 %collective-permute-start.25 = (bf16[4,240,576]{1,2,0:T(8,128)(2,1)S(1)}, bf16[4,240,576]{1,2,0:T(8,128)(2,1)}, u32[]{:S(2)}, u32[]{:S(2)}) collective-permute-start(bf16[4,240,576]{1,2,0:T(8,128)(2,1)S(1)} %copy.25), channel_id=1, source_target_pairs={{0,8},{8,0},{16,24},{24,16},{1,9},{9,1},{17,25},{25,17},{2,10},{10... | collective-permute-start | bytes 3317768 | tf_op jit(solution)/shard_map/ppermute | solution.py:43
  149.9 19.0 %collective-permute-start.40 = (bf16[4,240,576]{1,2,0:T(8,128)(2,1)}, bf16[4,240,576]{1,2,0:T(8,128)(2,1)}, u32[]{:S(2)}, u32[]{:S(2)}) collective-permute-start(bf16[4,240,576]{1,2,0:T(8,128)(2,1)} %copy.29), channel_id=1, source_target_pairs={{0,8},{8,0},{16,24},{24,16},{1,9},{9,1},{17,25},{25,17},{2,10},{10... | collective-permute-start | bytes 3317768 | tf_op jit(solution)/shard_map/ppermute | solution.py:43
  157.0 28.5 %collective-permute-start.41 = (bf16[4,240,576]{1,2,0:T(8,128)(2,1)}, bf16[4,240,576]{1,2,0:T(8,128)(2,1)}, u32[]{:S(2)}, u32[]{:S(2)}) collective-permute-start(bf16[4,240,576]{1,2,0:T(8,128)(2,1)} %copy.31), channel_id=1, source_target_pairs={{0,1},{1,0},{2,3},{3,2},{4,5},{5,4},{6,7},{7,6},{8,9},{9,8},{10,11... | collective-permute-start | bytes 3317768 | tf_op jit(solution)/shard_map/ppermute | solution.py:43
  161.2 35.8 %collective-permute-start.22 = (bf16[576,512]{1,0:T(8,128)(2,1)}, bf16[576,512]{1,0:T(8,128)(2,1)}, u32[]{:S(2)}, u32[]{:S(2)}) collective-permute-start(bf16[576,512]{1,0:T(8,128)(2,1)} %get-tuple-element.102.refs_0_), channel_id=1, source_target_pairs={{0,16},{8,24},{16,0},{24,8},{1,17},{9,25},{17,1},{25,9},{2,18},{10... | collective-permute-start | bytes 1769480 | tf_op jit(solution)/shard_map/ppermute | solution.py:43
  162.4 34.5 %collective-permute-start.46 = (bf16[2,96,576]{2,1,0:T(8,128)(2,1)}, bf16[2,96,576]{2,1,0:T(8,128)(2,1)}, u32[]{:S(2)}, u32[]{:S(2)}) collective-permute-start(bf16[2,96,576]{2,1,0:T(8,128)(2,1)} %slice.61), channel_id=1, source_target_pairs={{0,2},{1,3},{2,0},{3,1},{4,6},{5,7},{6,4},{7,5},{8,10},{9,11},{10,... | collective-permute-start | bytes 663560 | tf_op jit(solution)/shard_map/ppermute | solution.py:43
  168.9 22.2 %collective-permute-start.34 = (bf16[4,72,512]{2,1,0:T(8,128)(2,1)}, bf16[4,72,512]{2,1,0:T(8,128)(2,1)S(1)}, u32[]{:S(2)}, u32[]{:S(2)}) collective-permute-start(bf16[4,72,512]{2,1,0:T(8,128)(2,1)} %get-tuple-element.123), channel_id=1, source_target_pairs={{0,8},{8,0},{16,24},{24,16},{1,9},{9,1},{17,25},{25,17},{2,10},{10... | collective-permute-start | bytes 884744 | tf_op jit(solution)/shard_map/ppermute | solution.py:43
  171.6 26.8 %collective-permute-start.33 = (bf16[4,72,512]{2,1,0:T(8,128)(2,1)}, bf16[4,72,512]{2,1,0:T(8,128)(2,1)}, u32[]{:S(2)}, u32[]{:S(2)}) collective-permute-start(bf16[4,72,512]{2,1,0:T(8,128)(2,1)} %get-tuple-element.121), channel_id=1, source_target_pairs={{0,8},{8,0},{16,24},{24,16},{1,9},{9,1},{17,25},{25,17},{2,10},{10... | collective-permute-start | bytes 884744 | tf_op jit(solution)/shard_map/ppermute | solution.py:43
  196.9 40.7 %collective-permute-start.21 = (bf16[576,512]{1,0:T(8,128)(2,1)}, bf16[576,512]{1,0:T(8,128)(2,1)}, u32[]{:S(2)}, u32[]{:S(2)}) collective-permute-start(bf16[576,512]{1,0:T(8,128)(2,1)} %get-tuple-element.102.refs_0_), channel_id=1, source_target_pairs={{0,8},{8,0},{16,24},{24,16},{1,9},{9,1},{17,25},{25,17},{2,10},{10... | collective-permute-start | bytes 1769480 | tf_op jit(solution)/shard_map/ppermute | solution.py:43
  196.9 43.3 %collective-permute-start.23 = (bf16[576,512]{1,0:T(8,128)(2,1)}, bf16[576,512]{1,0:T(8,128)(2,1)}, u32[]{:S(2)}, u32[]{:S(2)}) collective-permute-start(bf16[576,512]{1,0:T(8,128)(2,1)} %collective-permute-done.22.refs_2_), channel_id=1, source_target_pairs={{0,8},{8,0},{16,24},{24,16},{1,9},{9,1},{17,25},{25,17},{2,10},{10... | collective-permute-start | bytes 1769480 | tf_op jit(solution)/shard_map/ppermute | solution.py:43
  198.5 31.1 %collective-permute-start.31 = (bf16[576,512]{1,0:T(8,128)(2,1)}, bf16[576,512]{1,0:T(8,128)(2,1)}, u32[]{:S(2)}, u32[]{:S(2)}) collective-permute-start(bf16[576,512]{1,0:T(8,128)(2,1)} %shard_map.211.refs_0_), channel_id=1, source_target_pairs={{0,16},{8,24},{16,0},{24,8},{1,17},{9,25},{17,1},{25,9},{2,18},{10... | collective-permute-start | bytes 1769480 | tf_op jit(solution)/shard_map/ppermute | solution.py:43
  210.0 16.5 %collective-permute-start.43 = (bf16[1,240,576]{2,1,0:T(8,128)(2,1)S(1)}, bf16[1,240,576]{2,1,0:T(8,128)(2,1)S(1)}, u32[]{:S(2)}, u32[]{:S(2)}) collective-permute-start(bf16[1,240,576]{2,1,0:T(8,128)(2,1)S(1)} %slice.75), channel_id=1, source_target_pairs={{0,4},{1,5},{2,6},{3,7},{4,0},{5,1},{6,2},{7,3},{8,12},{9,13},{10,... | collective-permute-start | bytes 829448 | tf_op jit(solution)/shard_map/ppermute | solution.py:43
  (55 other events, 592.0 us)
